TPU v7x, 32 devices: a whole 2x2x4 slice. The times are simulated.
32 devices in a mesh: user: 8 (over y, x, core), item: 4 (over z).
Axes of the slice: x: 2, y: 2, z: 4, core: 2. Of those that a mesh axis runs over, the one named last changes fastest.
Arguments:
- ratings: bfloat16 [6144, 6144], P('user', 'item')
- presence: int32 [48, 48], P('user', 'item'), may hold values from 0 to 1
- user_factors: float32 [6144, 128], P('user'), may hold values from -4 to 4
- item_factors: float32 [6144, 128], P('item'), may hold values from -4 to 4
- step_sizes: float32 [2], replicated, may hold values from 0.3 to 0.7
Outputs:
- new_users: float32 [6144, 128], P('user')
- new_items: float32 [6144, 128], P('item')
All inputs are finite; a program needn't handle non-finite values.
Results may differ from a plain program's by a relative error of at most 0.0003.
Values sent between devices are 32-bit elements; how exact they have to be, the bound alone decides.
A program may use at most 64 MiB of HBM per device.

v0:
```python
import jax
import jax.numpy as jnp
from jax import lax
from jax.sharding import PartitionSpec as P

BLK = 128


highest = lax.Precision.HIGHEST


def residual(ratings, presence, users, item_factors):
    predicted = lax.dot_general(
        users,
        item_factors,
        (((1,), (1,)), ((), ())),
        precision=highest,
        preferred_element_type=jnp.float32,
    )
    user_count, item_count = ratings.shape
    blocked = (ratings.astype(jnp.float32) - predicted).reshape(
        user_count // BLK, BLK, item_count // BLK, BLK
    )
    blocked = blocked * presence.astype(jnp.float32)[:, None, :, None]
    return blocked.reshape(user_count, item_count)


def user_partial(ratings, presence, users, item_factors):
    resid = residual(ratings, presence, users, item_factors)
    return jnp.dot(resid, item_factors, precision=highest, preferred_element_type=jnp.float32)


def body(ratings, presence, user_factors, item_factors, step_sizes):
    row_counts = jnp.repeat(jnp.sum(presence, axis=1).astype(jnp.float32), BLK)
    col_counts = jnp.repeat(jnp.sum(presence, axis=0).astype(jnp.float32), BLK)
    users = user_factors
    partial_value = user_partial(ratings, presence, users, item_factors)
    summed, counts = lax.psum((partial_value, row_counts), "item")
    scaling = step_sizes[0] / (BLK * (1.0 + counts))
    users = users + summed * scaling[:, None]
    partial_value = user_partial(ratings, presence, users, item_factors)
    summed = lax.psum(partial_value, "item")
    users = users + summed * scaling[:, None]
    resid = residual(ratings, presence, users, item_factors)
    item_part = lax.dot_general(
        resid,
        users,
        (((0,), (0,)), ((), ())),
        precision=highest,
        preferred_element_type=jnp.float32,
    )
    share = item_factors.shape[0] // lax.axis_size("user")
    start = lax.axis_index("user") * share
    summed, counts = (
        lax.psum_scatter(item_part, "user", scatter_dimension=0, tiled=True),
        lax.psum_scatter(col_counts, "user", scatter_dimension=0, tiled=True),
    )
    scaling = step_sizes[1] / (BLK * (1.0 + counts))
    owned = lax.dynamic_slice_in_dim(item_factors, start, share, 0) + summed * scaling[:, None]
    new_items = lax.all_gather(owned, "user", axis=0, tiled=True)
    return (users, new_items)


def solution(mesh):
    return jax.shard_map(
        body,
        mesh=mesh,
        in_specs=(P("user", "item"), P("user", "item"), P("user", None), P("item", None), P()),
        out_specs=(P("user", None), P("item", None)),
        check_vma=False,
    )
```

profile of v0, /device:TPU:0, one launch (start us, length us, event | category | flops | bytes accessed | tf_op | source)
XLA Modules:
  0.0 181.7 jit_solution(14713787341933128574)
XLA Ops:
  7.2 0.0 all-reduce.4.cloned.1.call-start
  7.2 0.9 fusion.18
  8.1 5.4 %fusion.20 = f32[768,1536]{1,0:T(8,128)S(1)} fusion(f32[768,128]{1,0:T(8,128)} %param.7, f32[1536,128]{1,0:T(8,128)} %param.8), kind=kOutput, calls=%fused_computation.27 | convolution fusion | flops 1811939328 | bytes 5898240 | tf_op jit(solution)/shard_map/dot_general | solution.py:13
  13.5 0.5 mul.62
  14.0 2.7 %copy-done = f32[6,128,12,128]{3,2,1,0:T(8,128)} copy-done((f32[6,128,12,128]{3,2,1,0:T(8,128)}, f32[6,128,12,128]{3,2,1,0:T(8,128)S(1)}, u32[]{:S(2)}) %copy-start) | copy-done | bytes 4718616
  16.6 5.9 %fusion.1 = f32[768,128]{1,0:T(8,128)} fusion(f32[1536,128]{1,0:T(8,128)S(1)} %copy-done.3, f32[768,1536]{1,0:T(8,128)S(1)} %fusion.20, bf16[768,1536]{1,0:T(8,128)(2,1)S(1)} %copy-done.2, f32[96,8,12,128]{3,2,1,0:T(8,128)S(1)} %bitcast.30), kind=kOutput, calls=%fused_computation.4 | convolution fusion | flops 1815478272 | bytes 12976128 | tf_op jit(solution)/shard_map/dot_general | solution.py:30
  22.5 0.0 all-reduce.4.cloned.1.call-update
  22.5 0.0 all-reduce.6.cloned.1.call-start
  22.6 0.1 broadcast_bitcast_fusion.1
  22.7 13.4 %psum.22 = f32[768]{0:T(1024)S(1)} all-reduce(f32[768]{0:T(1024)S(1)} %broadcast_bitcast_fusion.1), channel_id=1, replica_groups=mesh['user'=8,'item'=4] {'item'}, use_global_device_ids=true, to_apply=%region_2.0 | all-reduce | flops 768 | bytes 6144 | tf_op jit(solution)/shard_map/psum | solution.py:38
  36.1 0.6 fusion.19
  36.7 0.7 multiply_divide_fusion
  37.3 25.1 %all-reduce.4.cloned.1.call-done = f32[768,128]{1,0:T(8,128)} async-done(((f32[768,128]{1,0:T(8,128)}), f32[768,128]{1,0:T(8,128)}) %all-reduce.4.cloned.1.call-update) | async-done | bytes 393232 | tf_op jit(solution)/shard_map/psum | solution.py:38
  62.5 5.1 %fusion.15 = f32[768,1536]{1,0:T(8,128)S(1)} fusion(f32[1536,128]{1,0:T(8,128)S(1)} %copy-done.3, f32[768,128]{1,0:T(8,128)S(1)} %copy-done.5, f32[768,128]{1,0:T(8,128)} %all-reduce.4.cloned.1.call-done, f32[768]{0:T(1024)S(1)} %multiply_divide_fusion), kind=kOutput, calls=%fused_computation.18 | convolution fusion | flops 1812135936 | bytes 6294528 | tf_op jit(solution)/shard_map/dot_general | solution.py:13
  67.6 5.9 %fusion.4 = f32[768,128]{1,0:T(8,128)} fusion(f32[1536,128]{1,0:T(8,128)S(1)} %copy-done.3, f32[768,1536]{1,0:T(8,128)S(1)} %fusion.15, bf16[768,1536]{1,0:T(8,128)(2,1)S(1)} %copy-done.2, f32[96,8,12,128]{3,2,1,0:T(8,128)S(1)} %bitcast.32), kind=kOutput, calls=%fused_computation.6 | convolution fusion | flops 1815478272 | bytes 12976128 | tf_op jit(solution)/shard_map/dot_general | solution.py:30
  73.5 0.0 all-reduce.6.cloned.1.call-update
  73.5 0.3 reduce-scatter.2.cloned.1.call-start
  73.8 36.5 %all-reduce.6.cloned.1.call-done = f32[768,128]{1,0:T(8,128)} async-done(((f32[768,128]{1,0:T(8,128)}), f32[768,128]{1,0:T(8,128)}) %all-reduce.6.cloned.1.call-update) | async-done | bytes 393232 | tf_op jit(solution)/shard_map/psum | solution.py:42
  110.3 1.4 multiply_add_fusion
  111.7 0.0 copy-start.4
  111.7 4.0 %fusion.21 = f32[768,1536]{1,0:T(8,128)S(1)} fusion(f32[768,128]{1,0:T(8,128)S(1)} %multiply_add_fusion, f32[1536,128]{1,0:T(8,128)S(1)} %copy-done.3), kind=kOutput, calls=%fused_computation.28 | convolution fusion | flops 1811939328 | bytes 5898240 | tf_op jit(solution)/shard_map/dot_general | solution.py:13
  115.7 0.0 copy-start.7
  115.7 12.4 %fusion.7 = f32[1536,128]{1,0:T(8,128)} fusion(f32[768,128]{1,0:T(8,128)S(1)} %multiply_add_fusion, f32[768,1536]{1,0:T(8,128)S(1)} %fusion.21, bf16[768,1536]{1,0:T(8,128)(2,1)S(1)} %copy-done.2, f32[96,8,12,128]{3,2,1,0:T(8,128)} %bitcast.31), kind=kOutput, calls=%fused_computation.8 | convolution fusion | flops 1815478272 | bytes 12976128 | tf_op jit(solution)/shard_map/dot_general | solution.py:45
  128.1 0.0 reduce-scatter.2.cloned.1.call-update
  128.2 0.6 dynamic-slice
  129.3 0.1 broadcast_bitcast_fusion
  129.4 12.1 %all-reduce = f32[1536]{0:T(1024)S(1)} all-reduce(f32[1536]{0:T(1024)S(1)} %broadcast_bitcast_fusion), channel_id=3, replica_groups=mesh['user'=8,'item'=4] {'user'}, use_global_device_ids=true, to_apply=%region_6.0.clone | all-reduce | flops 1536 | bytes 12288
  141.5 0.7 fusion.17
  142.2 20.7 %reduce-scatter.2.cloned.1.call-done = f32[192,128]{1,0:T(8,128)} async-done(((f32[1536,128]{1,0:T(8,128)}), f32[192,128]{1,0:T(8,128)}) %reduce-scatter.2.cloned.1.call-update) | async-done | bytes 98320 | tf_op jit(solution)/shard_map/reduce_scatter | solution.py:55
  162.9 1.0 multiply_add_fusion.2
  163.9 10.3 %all_gather.3 = f32[1536,128]{1,0:T(8,128)S(1)} all-gather(f32[192,128]{1,0:T(8,128)S(1)} %multiply_add_fusion.2), channel_id=1, replica_groups=mesh['user'=8,'item'=4] {'user'}, dimensions={0}, use_global_device_ids=true | all-gather | bytes 884736 | tf_op jit(solution)/shard_map/all_gather | solution.py:60
  174.2 0.9 copy.23
  (15 shorter events, 0.0 us)
Async XLA Ops:
  7.2 55.3 %all-reduce.4.cloned.1.call-start = ((), (), s32[]{:S(2)}) async-start(), calls=%async_computation.1 | async-start | bytes 786432 | tf_op jit(solution)/shard_map/psum | solution.py:38
  8.1 8.5 %copy-start.2 = (bf16[768,1536]{1,0:T(8,128)(2,1)S(1)}, bf16[768,1536]{1,0:T(8,128)(2,1)}, u32[]{:S(2)}) copy-start(bf16[768,1536]{1,0:T(8,128)(2,1)} %param.5) | copy-start | bytes 7077892
  8.1 8.5 %copy-start.3 = (f32[1536,128]{1,0:T(8,128)S(1)}, f32[1536,128]{1,0:T(8,128)}, u32[]{:S(2)}) copy-start(f32[1536,128]{1,0:T(8,128)} %param.8) | copy-start | bytes 2359300
  14.0 2.7 %copy-start = (f32[6,128,12,128]{3,2,1,0:T(8,128)}, f32[6,128,12,128]{3,2,1,0:T(8,128)S(1)}, u32[]{:S(2)}) copy-start(f32[6,128,12,128]{3,2,1,0:T(8,128)S(1)} %mul.62) | copy-start | bytes 14155780
  16.6 19.4 %copy-start.6 = (f32[2]{0:T(128)S(1)}, f32[2]{0:T(128)}, u32[]{:S(2)}) copy-start(f32[2]{0:T(128)} %param.9) | copy-start | bytes 28
  16.6 45.8 %copy-start.5 = (f32[768,128]{1,0:T(8,128)S(1)}, f32[768,128]{1,0:T(8,128)}, u32[]{:S(2)}) copy-start(f32[768,128]{1,0:T(8,128)} %param.7) | copy-start | bytes 1179652
  22.5 87.8 %all-reduce.6.cloned.1.call-start = ((), (), s32[]{:S(2)}) async-start(), calls=%async_computation.2 | async-start | bytes 786432 | tf_op jit(solution)/shard_map/psum | solution.py:42
  62.5 5.1 %copy-start.1 = (f32[6,128,12,128]{3,2,1,0:T(8,128)S(1)}, f32[6,128,12,128]{3,2,1,0:T(8,128)}, u32[]{:S(2)}) copy-start(f32[6,128,12,128]{3,2,1,0:T(8,128)} %copy-done) | copy-start | bytes 14155780
  73.5 89.4 %reduce-scatter.2.cloned.1.call-start = ((), (), s32[]{:S(2)}) async-start(), calls=%async_computation.3 | async-start | bytes 884736 | tf_op jit(solution)/shard_map/reduce_scatter | solution.py:55
  111.7 16.4 %copy-start.4 = (f32[768,128]{1,0:T(8,128)}, f32[768,128]{1,0:T(8,128)S(1)}, u32[]{:S(2)}) copy-start(f32[768,128]{1,0:T(8,128)S(1)} %multiply_add_fusion) | copy-start | bytes 1179652
  115.7 12.5 %copy-start.7 = (u32[32]{0:T(128)S(1)}, u32[32]{0:T(128)}, u32[]{:S(2)}) copy-start(u32[32]{0:T(128)} %constant.21) | copy-start | bytes 388
Sparse Core Ops, SparseCore 0:
  22.6 39.7 all-reduce.3
  73.6 36.6 all-reduce.5
  128.3 34.6 reduce-scatter.1
where the time goes:
time: 182 us
  waiting for transfers between devices  82.4 us (45%)
  matrix products  38.6 us (21%)
  blocking collectives  35.9 us (20%)
  between operations  14.5 us (8%)
  local copies, waits for them, and re-layouts  5.36 us (3%)
  other arithmetic  4.64 us (3%)
    psum x1, waiting for transfers between devices, body(): summed = lax.psum(partial_value, 'item')  36.5 us
    psum x1, waiting for transfers between devices, body(): summed, counts = lax.psum((partial_value, row_counts), 'item')  25.1 us
    reduce_scatter x1, waiting for transfers between devices, body(): lax.psum_scatter(item_part, 'user', scatter_dimension=0, tiled=True)  20.7 us
    dot_general x3, matrix products, residual(): lax.dot_general(users, item_factors, (((1,), (1,)), ((), ())), precision=...  14.5 us
    psum x1, blocking collectives, body(): summed, counts = lax.psum((partial_value, row_counts), 'item')  13.4 us
    dot_general x1, matrix products, body(): lax.dot_general(resid, users, (((0,), (0,)), ((), ())), precision=highest...  12.4 us
    unnamed x1, blocking collectives  12.1 us
    dot_general x2, matrix products, user_partial(): jnp.dot(resid, item_factors, precision=highest, preferred_element_type=jn...  11.7 us
  transfers between devices with their start and end apart: 3, of which 3 were waited for; matrix products, arithmetic and copies ran while one was open for 1% of the time, Pallas kernels for 0%

commit v1 on v0

v1 whole, which is shorter than its diff:
```python
import functools

import jax
import jax.numpy as jnp
from jax import lax
from jax.experimental import pallas as pl
from jax.experimental.pallas import tpu as pltpu
from jax.sharding import PartitionSpec as P

BLK = 128
f32 = jnp.float32
bf16 = jnp.bfloat16
MESH = pl.DeviceIdType.MESH


def split(x):
    hi = x.astype(bf16)
    lo = (x - hi.astype(f32)).astype(bf16)
    return hi, lo


def both(x):
    return jnp.concatenate(split(x), axis=1)


def fold(x):
    k = x.shape[1] // 2
    return x[:, :k] + x[:, k:]


def dot3(x, y):
    xh, xl = split(x)
    yh, yl = split(y)
    return jnp.dot(
        jnp.concatenate([xh, xl, xh], axis=1),
        jnp.concatenate([yh, yh, yl], axis=0),
        preferred_element_type=f32,
    )


def gram(pair):
    full = lax.dot_general(pair, pair, (((0,), (0,)), ((), ())), preferred_element_type=f32)
    k = full.shape[0] // 2
    full = full[:k] + full[k:]
    return full[:, :k] + full[:, k:]


def kernel(
    nu,
    ni,
    r_ref,
    p_ref,
    u_ref,
    q_ref,
    step_ref,
    ou_ref,
    oi_ref,
    qq,
    qg,
    masked,
    masked_t,
    mask_row,
    part,
    rs_in,
    pp,
    hs,
    acc,
    scale,
    cc_out,
    cc_in,
    *rest,
):
    levels = nu.bit_length() - 1
    halves = rest[:levels]
    (rs_s, rs_r, ag_s, ag_r, cc_s, cc_r, hv_s, hv_r, db_s, db_r) = rest[levels:]
    ub, _, k = u_ref.shape
    items = q_ref.shape[0]
    ib = items // BLK
    h = ub // 2
    u = lax.axis_index("user")
    z = lax.axis_index("item")

    barrier = pltpu.get_barrier_semaphore()
    for d in range(1, nu):
        pl.semaphore_signal(barrier, inc=1, device_id=(lax.rem(u + d, nu), z), device_id_type=MESH)

    @pl.when(z > 0)
    def _():
        pl.semaphore_signal(barrier, inc=1, device_id=(u, z - 1), device_id_type=MESH)

    @pl.when(z < ni - 1)
    def _():
        pl.semaphore_signal(barrier, inc=1, device_id=(u, z + 1), device_id_type=MESH)

    def rs_copy(b, to):
        return pltpu.make_async_remote_copy(
            src_ref=part.at[b],
            dst_ref=rs_in.at[b],
            send_sem=rs_s.at[b],
            recv_sem=rs_r.at[b],
            device_id=(u, to),
            device_id_type=MESH,
        )

    def ag_copy(b, to):
        return pltpu.make_async_remote_copy(
            src_ref=ou_ref.at[b],
            dst_ref=ou_ref.at[b],
            send_sem=ag_s.at[b],
            recv_sem=ag_r.at[b],
            device_id=(u, to),
            device_id_type=MESH,
        )

    def cc_copy(d):
        return pltpu.make_async_remote_copy(
            src_ref=cc_out,
            dst_ref=cc_in.at[d - 1],
            send_sem=cc_s.at[d - 1],
            recv_sem=cc_r.at[d - 1],
            device_id=(lax.rem(u + d, nu), z),
            device_id_type=MESH,
        )

    left = jnp.maximum(z - 1, 0)
    right = jnp.minimum(z + 1, ni - 1)

    @pl.loop(0, ib)
    def _(i):
        rows = pl.ds(pl.multiple_of(i * BLK, BLK), BLK)
        pair = both(q_ref[rows, :])
        qq[rows, :] = pair
        qg[i] = gram(pair)
        hs[i] = jnp.zeros((k, k), f32)
        count = p_ref[0, i]
        for b in range(1, ub):
            count = count + p_ref[b, i]
        cc_out[pl.ds(i, 1), :] = jnp.full((1, k), count.astype(f32), f32)

    pl.semaphore_wait(barrier, nu - 1 + jnp.minimum(z, 1) + jnp.minimum(ni - 1 - z, 1))

    @pl.loop(0, ub)
    def _(m):
        b = m // 2 + (m % 2) * h
        rows = pl.ds(pl.multiple_of(b * BLK, BLK), BLK)
        total = p_ref[b, 0]
        grams = jnp.zeros((k, k), f32)
        for i in range(ib):
            present = p_ref[b, i].astype(f32)
            mask_row[:, i * BLK : (i + 1) * BLK] = jnp.full((8, BLK), present, f32)
            grams = grams + present * qg[i]
            if i:
                total = total + p_ref[b, i]
        kept = r_ref[rows, :] * mask_row[0:1, :].astype(bf16)
        masked[b] = kept
        part[b, 0:BLK] = fold(jnp.dot(kept, qq[...], preferred_element_type=f32))
        part[b, BLK : BLK + k] = grams
        part[b, BLK + k : BLK + k + 8] = jnp.full((8, k), total.astype(f32), f32)

        @pl.when(jnp.logical_and(z == ni - 1, b < h))
        def _():
            rs_copy(b, left).start()

        @pl.when(jnp.logical_and(z == 0, b >= h))
        def _():
            rs_copy(b, right).start()

    for d in range(1, nu):
        cc_copy(d).start()

    def finish(b):
        a = part[b, 0:BLK]
        g = part[b, BLK : BLK + k]
        s = step_ref[0] / (BLK * (1.0 + part[b, BLK + k : BLK + k + 1]))
        p = u_ref[b]
        p = p + s * (a - dot3(p, g))
        p = p + s * (a - dot3(p, g))
        ou_ref[b] = p

    def use(b):
        pair = both(ou_ref[b])
        pp[pl.ds(pl.multiple_of(b * BLK, BLK), BLK), :] = pair
        g = gram(pair)
        for i in range(ib):
            hs[i] = hs[i] + p_ref[b, i].astype(f32) * g

    def reduce_step(j, b, frm, to, away, last):
        @pl.when(jnp.logical_and(away, jnp.logical_and(j >= 0, j < h)))
        def _():
            rs_copy(b, frm).wait_recv()
            part[b] = part[b] + rs_in[b]

            @pl.when(jnp.logical_not(last))
            def _():
                rs_copy(b, to).start()

            @pl.when(last)
            def _():
                finish(b)
                ag_copy(b, frm).start()
                use(b)

    def gather_step(j, b, frm, to, away, last):
        @pl.when(jnp.logical_and(away, jnp.logical_and(j >= 0, j < h)))
        def _():
            ag_copy(b, frm).wait_recv()

            @pl.when(jnp.logical_not(last))
            def _():
                ag_copy(b, to).start()

            use(b)

    def transpose_block(b):
        masked_t[:, pl.ds(pl.multiple_of(b * BLK, BLK), BLK)] = masked[b].T

    steps = 2 * (ni - 1) + h
    first, end = z == 0, z == ni - 1
    inner_first, inner_end = z > 0, z < ni - 1

    @pl.loop(1, steps)
    def _(t):
        j = t - z
        reduce_step(j, jnp.clip(j, 0, h - 1) + h, left, right, inner_first, end)
        j = t - (ni - 1 - z)
        reduce_step(j, jnp.clip(j, 0, h - 1), right, left, inner_end, first)
        j = t - (ni - 1) - z
        gather_step(j, jnp.clip(j, 0, h - 1), left, right, inner_first, end)
        j = t - 2 * (ni - 1) + z
        gather_step(j, jnp.clip(j, 0, h - 1) + h, right, left, inner_end, first)

        @pl.when(t - 1 < ub)
        def _():
            transpose_block(jnp.minimum(t - 1, ub - 1))

    for b in range(steps - 1, ub):
        transpose_block(b)

    bits = [(u // (1 << i)) % 2 for i in range(levels)]
    partners = [u + (1 << i) * (1 - 2 * bits[i]) for i in range(levels)]
    core = bits[0]

    def pick(xs, level):
        if level == 0:
            return xs[0]
        one, two = xs[level], xs[levels - level]
        return one + core * (two - one)

    size = items
    start = 0
    plan = []
    for level in range(levels):
        size = size // 2
        bit = pick(bits, level)
        keep = pl.multiple_of(start + bit * size, 8)
        send = pl.multiple_of(start + (1 - bit) * size, 8)
        plan.append((size, keep, send, pick(partners, level)))
        start = keep

    def half_copy(level):
        n, _, send, to = plan[level]
        return pltpu.make_async_remote_copy(
            src_ref=acc.at[pl.ds(send, n)],
            dst_ref=halves[level],
            send_sem=hv_s.at[level],
            recv_sem=hv_r.at[level],
            device_id=(to, z),
            device_id_type=MESH,
        )

    def double_copy(level):
        n, keep, _, to = plan[level]
        return pltpu.make_async_remote_copy(
            src_ref=oi_ref.at[pl.ds(keep, n)],
            dst_ref=oi_ref.at[pl.ds(keep, n)],
            send_sem=db_s.at[level],
            recv_sem=db_r.at[level],
            device_id=(to, z),
            device_id_type=MESH,
        )

    def product(base, n):
        rows = pl.ds(pl.multiple_of(base, BLK), n)
        acc[rows, :] = fold(jnp.dot(masked_t[rows, :], pp[...], preferred_element_type=f32))
        for m in range(n // BLK):
            block = base // BLK + m
            own = pl.ds(pl.multiple_of(base + m * BLK, BLK), BLK)
            acc[own, :] = acc[own, :] - dot3(q_ref[own, :], hs[block])

    n, keep, send, _ = plan[0]
    product(send, n)
    half_copy(0).start()
    product(keep, n)

    for d in range(1, nu):
        cc_copy(d).wait_recv()
    counts = cc_out[...]
    for d in range(1, nu):
        counts = counts + cc_in[d - 1]
    scaling = step_ref[1] / (BLK * (1.0 + counts))
    for i in range(ib):
        scale[i * BLK : (i + 1) * BLK, :] = jnp.broadcast_to(scaling[i : i + 1], (BLK, k))

    for level in range(levels):
        n, keep, _, _ = plan[level]
        if level:
            half_copy(level).start()
        half_copy(level).wait_recv()
        rows = pl.ds(keep, n)
        if level < levels - 1:
            acc[rows, :] = acc[rows, :] + halves[level][...]
        else:
            oi_ref[rows, :] = q_ref[rows, :] + (acc[rows, :] + halves[level][...]) * scale[rows, :]

    for level in reversed(range(levels)):
        double_copy(level).start()
        n, keep, send, to = plan[level]
        double_copy(level).wait_recv()

    for level in range(levels):
        half_copy(level).wait_send()
        double_copy(level).wait_send()
    for d in range(1, nu):
        cc_copy(d).wait_send()

    @pl.loop(0, h)
    def _(b):
        @pl.when(z > 0)
        def _():
            rs_copy(b, left).wait_send()
            ag_copy(b + h, left).wait_send()

        @pl.when(z < ni - 1)
        def _():
            rs_copy(b + h, right).wait_send()
            ag_copy(b, right).wait_send()


def solution(mesh):
    nu, ni = mesh.shape["user"], mesh.shape["item"]

    def body(ratings, presence, user_factors, item_factors, step_sizes):
        users, items = ratings.shape
        k = item_factors.shape[1]
        ub, ib = users // BLK, items // BLK
        levels = nu.bit_length() - 1
        ibp = -(-ib // 8) * 8
        vm = pl.BlockSpec(memory_space=pltpu.VMEM)
        sm = pl.BlockSpec(memory_space=pltpu.SMEM)
        dma = pltpu.SemaphoreType.DMA
        new_users, new_items = pl.pallas_call(
            functools.partial(kernel, nu, ni),
            out_shape=(
                jax.ShapeDtypeStruct((ub, BLK, k), f32),
                jax.ShapeDtypeStruct((items, k), f32),
            ),
            in_specs=[vm, sm, vm, vm, sm],
            out_specs=(vm, vm),
            scratch_shapes=[
                pltpu.VMEM((items, 2 * k), bf16),
                pltpu.VMEM((ib, k, k), f32),
                pltpu.VMEM((ub, BLK, items), bf16),
                pltpu.VMEM((items, users), bf16),
                pltpu.VMEM((8, items), f32),
                pltpu.VMEM((ub, BLK + k + 8, k), f32),
                pltpu.VMEM((ub, BLK + k + 8, k), f32),
                pltpu.VMEM((users, 2 * k), bf16),
                pltpu.VMEM((ib, k, k), f32),
                pltpu.VMEM((items, k), f32),
                pltpu.VMEM((items, k), f32),
                pltpu.VMEM((ibp, k), f32),
                pltpu.VMEM((nu - 1, ibp, k), f32),
            ]
            + [pltpu.VMEM((items >> (i + 1), k), f32) for i in range(levels)]
            + [
                dma((ub,)),
                dma((ub,)),
                dma((ub,)),
                dma((ub,)),
                dma((nu - 1,)),
                dma((nu - 1,)),
                dma((levels,)),
                dma((levels,)),
                dma((levels,)),
                dma((levels,)),
            ],
            compiler_params=pltpu.CompilerParams(
                collective_id=0, has_side_effects=True, vmem_limit_bytes=40 * 2**20
            ),
            cost_estimate=pl.CostEstimate(
                flops=8 * users * items * k, bytes_accessed=2 * users * items, transcendentals=0
            ),
        )(ratings, presence, user_factors.reshape(ub, BLK, k), item_factors, step_sizes)
        return new_users.reshape(users, k), new_items

    return jax.shard_map(
        body,
        mesh=mesh,
        in_specs=(P("user", "item"), P("user", "item"), P("user", None), P("item", None), P()),
        out_specs=(P("user", None), P("item", None)),
        check_vma=False,
    )
```

time: 182 us -> 67.5 us (0.37)
  waiting for transfers between devices: 82.4 us -> 0 us
  Pallas kernels: 0 us -> 59 us
  matrix products: 38.6 us -> 0 us
  blocking collectives: 35.9 us -> 0 us
  between operations: 14.5 us -> 0.65 us
  other arithmetic: 4.64 us -> 0 us
    psum x2 -> x0, waiting for transfers between devices: 61.7 us -> none  [the longest x1 36.5 us: body(): summed = lax.psum(partial_value, 'item')]
    pallas_call x0 -> x1, Pallas kernels: none -> 59 us  [body(): pl.pallas_call(functools.partial(kernel, nu, ni), out_shape=(jax.ShapeDty...]
    dot_general x6 -> x0, matrix products: 38.6 us -> none  [the longest x3 14.5 us: residual(): lax.dot_general(users, item_factors, (((1,), (1,)), ((), ())), precision=...]
    reduce_scatter x1 -> x0, waiting for transfers between devices: 20.7 us -> none  [body(): lax.psum_scatter(item_part, 'user', scatter_dimension=0, tiled=True)]
    psum x1 -> x0, blocking collectives: 13.4 us -> none  [body(): summed, counts = lax.psum((partial_value, row_counts), 'item')]
    unnamed x1 -> x0, blocking collectives: 12.1 us -> none
    all_gather x1 -> x0, blocking collectives: 10.3 us -> none  [body(): new_items = lax.all_gather(owned, 'user', axis=0, tiled=True)]
    unnamed x18 -> x12, local copies, waits for them, and re-layouts: 4.14 us -> 6.75 us
  transfers between devices with their start and end apart: 3 -> 0, of which waited for: 3 -> 0; matrix products, arithmetic and copies ran while one was open for 1% -> 0% of each run, Pallas kernels for 0% -> 0%
where the time goes in v1:
time: 67.5 us; the launch traced here: 66.4 us
  Pallas kernels  59 us (87%)
  local copies, waits for them, and re-layouts  6.75 us (10%)
    pallas_call x1, Pallas kernels, body(): pl.pallas_call(functools.partial(kernel, nu, ni), out_shape=(jax.ShapeDty...  59 us
    unnamed x12, local copies, waits for them, and re-layouts  6.75 us

profile of v1, /device:TPU:0, one launch (start us, length us, event | category | flops | bytes accessed | tf_op | source)
XLA Modules:
  0.0 66.4 jit_solution(7303233973212998509)
XLA Ops:
  0.6 0.0 copy-start
  0.6 1.7 %copy-done = bf16[768,1536]{1,0:T(8,128)(2,1)S(1)} copy-done((bf16[768,1536]{1,0:T(8,128)(2,1)S(1)}, bf16[768,1536]{1,0:T(8,128)(2,1)}, u32[]{:S(2)}) %copy-start) | copy-done | bytes 2359320
  2.3 0.0 copy-start.1
  2.3 1.1 %copy-done.1 = f32[1536,128]{1,0:T(8,128)S(1)} copy-done((f32[1536,128]{1,0:T(8,128)S(1)}, f32[1536,128]{1,0:T(8,128)}, u32[]{:S(2)}) %copy-start.1) | copy-done | bytes 786456
  3.4 0.0 copy-start.2
  3.4 1.0 %copy-done.2 = f32[768,128]{1,0:T(8,128)S(1)} copy-done((f32[768,128]{1,0:T(8,128)S(1)}, f32[768,128]{1,0:T(8,128)}, u32[]{:S(2)}) %copy-start.2) | copy-done | bytes 393240
  4.4 0.0 copy-start.3
  4.4 0.7 %copy-done.3 = s32[6,12]{1,0:T(8,128)S(1)} copy-done((s32[6,12]{1,0:T(8,128)S(1)}, s32[6,12]{1,0:T(8,128)}, u32[]{:S(2)}) %copy-start.3) | copy-done | bytes 312
  5.1 0.0 copy-start.4
  5.1 0.7 copy-done.4
  5.8 59.0 %shard_map.68 = (f32[6,128,128]{2,1,0:T(8,128)S(1)}, f32[1536,128]{1,0:T(8,128)S(1)}) custom-call(bf16[768,1536]{1,0:T(8,128)(2,1)S(1)} %copy-done, s32[6,12]{1,0:T(8,128)S(1)} %copy-done.3, f32[6,128,128]{2,1,0:T(8,128)S(1)} %bitcast.3, f32[1536,128]{1,0:T(8,128)S(1)} %copy-done.1, f32[2]{0:T(128)S(1)} %copy-done.4), custom_call_target="tpu_custom_call" | custom-call | flops 1207959552 | bytes 2359296 | tf_op jit(solution)/shard_map/pallas_call | solution.py:351
  64.8 0.7 %copy.9 = f32[768,128]{1,0:T(8,128)} copy(f32[768,128]{1,0:T(8,128)S(1)} %bitcast.2) | data formatting | bytes 786432
  65.6 0.9 %copy.10 = f32[1536,128]{1,0:T(8,128)} copy(f32[1536,128]{1,0:T(8,128)S(1)} %get-tuple-element.9) | data formatting | bytes 1572864
Async XLA Ops:
  0.6 1.7 %copy-start = (bf16[768,1536]{1,0:T(8,128)(2,1)S(1)}, bf16[768,1536]{1,0:T(8,128)(2,1)}, u32[]{:S(2)}) copy-start(bf16[768,1536]{1,0:T(8,128)(2,1)} %r_ref.1) | copy-start | bytes 7077892
  2.3 1.1 %copy-start.1 = (f32[1536,128]{1,0:T(8,128)S(1)}, f32[1536,128]{1,0:T(8,128)}, u32[]{:S(2)}) copy-start(f32[1536,128]{1,0:T(8,128)} %q_ref.1) | copy-start | bytes 2359300
  3.4 1.0 %copy-start.2 = (f32[768,128]{1,0:T(8,128)S(1)}, f32[768,128]{1,0:T(8,128)}, u32[]{:S(2)}) copy-start(f32[768,128]{1,0:T(8,128)} %param.7) | copy-start | bytes 1179652
  4.4 0.7 %copy-start.3 = (s32[6,12]{1,0:T(8,128)S(1)}, s32[6,12]{1,0:T(8,128)}, u32[]{:S(2)}) copy-start(s32[6,12]{1,0:T(8,128)} %p_ref.1) | copy-start | bytes 868
  5.1 0.7 copy-start.4

commit v2 on v1

--- a/solution.py
+++ b/solution.py
@@ -45,16 +45,48 @@
     return full[:, :k] + full[:, k:]
 
 
+def grid_of(rows, k):
+    row = lax.broadcasted_iota(jnp.int32, (rows, k), 0)
+    lane = lax.broadcasted_iota(jnp.int32, (rows, k), 1)
+    return row, lane
+
+
+def pack(g):
+    k = g.shape[0]
+    n = k // 2
+    row, lane = grid_of(n, k)
+    low = g[n:]
+    packed = jnp.where(lane < row, pltpu.roll(low, n, 1), g[:n])
+    diagonal = jnp.sum(jnp.where(lane == row + n, low, 0.0), axis=0, keepdims=True)
+    return packed, diagonal
+
+
+def unpack(packed, diagonal):
+    n, k = packed.shape
+    row, lane = grid_of(n, k)
+    upper = jnp.where(lane > row, packed, 0.0)
+    lower = pltpu.roll(jnp.where(lane < row, packed, 0.0), n, 1)
+    once = jnp.concatenate([upper, lower], axis=0)
+    top = jnp.where(lane == row, packed, 0.0)
+    bottom = jnp.where(lane == row + n, diagonal, 0.0)
+    return once + once.T + jnp.concatenate([top, bottom], axis=0)
+
+
 def kernel(
     nu,
     ni,
+    r_hbm,
+    p_hbm,
+    u_hbm,
+    q_hbm,
+    step_hbm,
+    ou_ref,
+    oi_ref,
     r_ref,
     p_ref,
     u_ref,
     q_ref,
     step_ref,
-    ou_ref,
-    oi_ref,
     qq,
     qg,
     masked,
@@ -72,13 +104,38 @@
 ):
     levels = nu.bit_length() - 1
     halves = rest[:levels]
-    (rs_s, rs_r, ag_s, ag_r, cc_s, cc_r, hv_s, hv_r, db_s, db_r) = rest[levels:]
+    (in_s, row_s, rs_s, rs_r, ag_s, ag_r, cc_s, cc_r, hv_s, hv_r, db_s, db_r) = rest[levels:]
     ub, _, k = u_ref.shape
     items = q_ref.shape[0]
     ib = items // BLK
     h = ub // 2
+    half = BLK // 2
+    kh = k // 2
+    sub = part.shape[1]
+    cut = sub - kh - 8
     u = lax.axis_index("user")
     z = lax.axis_index("item")
+
+    inputs = [
+        pltpu.make_async_copy(src, dst, in_s.at[n])
+        for n, (src, dst) in enumerate(
+            ((q_hbm, q_ref), (p_hbm, p_ref), (step_hbm, step_ref), (u_hbm, u_ref))
+        )
+    ]
+    for copy in inputs:
+        copy.start()
+
+    def fetch(b):
+        rows = pl.ds(pl.multiple_of(b * BLK, BLK), BLK)
+        return pltpu.make_async_copy(r_hbm.at[rows], r_ref.at[b], row_s.at[b])
+
+    late = z // ((ni + 1) // 2)
+
+    def ordered(m):
+        return lax.rem(m + (1 - late) * h, ub)
+
+    for m in range(ub):
+        fetch(ordered(m)).start()
 
     barrier = pltpu.get_barrier_semaphore()
     for d in range(1, nu):
@@ -124,6 +181,9 @@
 
     left = jnp.maximum(z - 1, 0)
     right = jnp.minimum(z + 1, ni - 1)
+
+    for copy in inputs:
+        copy.wait()
 
     @pl.loop(0, ib)
     def _(i):
@@ -141,8 +201,7 @@
 
     @pl.loop(0, ub)
     def _(m):
-        b = m // 2 + (m % 2) * h
-        rows = pl.ds(pl.multiple_of(b * BLK, BLK), BLK)
+        b = ordered(m)
         total = p_ref[b, 0]
         grams = jnp.zeros((k, k), f32)
         for i in range(ib):
@@ -151,83 +210,115 @@
             grams = grams + present * qg[i]
             if i:
                 total = total + p_ref[b, i]
-        kept = r_ref[rows, :] * mask_row[0:1, :].astype(bf16)
+        fetch(b).wait()
+        kept = r_ref[b] * mask_row[0:1, :].astype(bf16)
         masked[b] = kept
-        part[b, 0:BLK] = fold(jnp.dot(kept, qq[...], preferred_element_type=f32))
-        part[b, BLK : BLK + k] = grams
-        part[b, BLK + k : BLK + k + 8] = jnp.full((8, k), total.astype(f32), f32)
+        a = fold(jnp.dot(kept, qq[...], preferred_element_type=f32))
+        packed, diagonal = pack(grams)
+        part[2 * b, 0:kh] = packed
+        part[2 * b, kh : kh + 1] = diagonal
+        part[2 * b, kh + 1 : kh + 8] = jnp.full((7, k), total.astype(f32), f32)
+        part[2 * b, kh + 8 : sub] = a[:cut]
+        part[2 * b + 1, 0 : BLK - cut] = a[cut:]
 
         @pl.when(jnp.logical_and(z == ni - 1, b < h))
         def _():
-            rs_copy(b, left).start()
+            rs_copy(2 * b, left).start()
+            rs_copy(2 * b + 1, left).start()
 
         @pl.when(jnp.logical_and(z == 0, b >= h))
         def _():
-            rs_copy(b, right).start()
+            rs_copy(2 * b, right).start()
+            rs_copy(2 * b + 1, right).start()
 
     for d in range(1, nu):
         cc_copy(d).start()
 
     def finish(b):
-        a = part[b, 0:BLK]
-        g = part[b, BLK : BLK + k]
-        s = step_ref[0] / (BLK * (1.0 + part[b, BLK + k : BLK + k + 1]))
+        a = jnp.concatenate([part[2 * b, kh + 8 : sub], part[2 * b + 1, 0 : BLK - cut]], axis=0)
+        g = unpack(part[2 * b, 0:kh], part[2 * b, kh : kh + 1])
+        gh, gl = split(g)
+        gs = jnp.concatenate([gh, gh, gl], axis=0)
+        s = step_ref[0] / (BLK * (1.0 + part[2 * b, kh + 1 : kh + 2]))
         p = u_ref[b]
-        p = p + s * (a - dot3(p, g))
-        p = p + s * (a - dot3(p, g))
-        ou_ref[b] = p
+        for _ in range(2):
+            ph, pl_ = split(p)
+            ps = jnp.concatenate([ph, pl_, ph], axis=1)
+            p = p + s * (a - jnp.dot(ps, gs, preferred_element_type=f32))
+        ou_ref[2 * b] = p[:half]
+        ou_ref[2 * b + 1] = p[half:]
 
     def use(b):
-        pair = both(ou_ref[b])
+        pair = both(jnp.concatenate([ou_ref[2 * b], ou_ref[2 * b + 1]], axis=0))
         pp[pl.ds(pl.multiple_of(b * BLK, BLK), BLK), :] = pair
         g = gram(pair)
         for i in range(ib):
             hs[i] = hs[i] + p_ref[b, i].astype(f32) * g
 
-    def reduce_step(j, b, frm, to, away, last):
-        @pl.when(jnp.logical_and(away, jnp.logical_and(j >= 0, j < h)))
-        def _():
-            rs_copy(b, frm).wait_recv()
-            part[b] = part[b] + rs_in[b]
+    def valid(j, away):
+        return jnp.logical_and(away, jnp.logical_and(j >= 0, j < 2 * h))
+
+    def reduce_step(j, c, frm, to, away, last):
+        @pl.when(valid(j, away))
+        def _():
+            rs_copy(c, frm).wait_recv()
+            part[c] = part[c] + rs_in[c]
 
             @pl.when(jnp.logical_not(last))
             def _():
-                rs_copy(b, to).start()
-
-            @pl.when(last)
-            def _():
-                finish(b)
-                ag_copy(b, frm).start()
-                use(b)
-
-    def gather_step(j, b, frm, to, away, last):
-        @pl.when(jnp.logical_and(away, jnp.logical_and(j >= 0, j < h)))
-        def _():
-            ag_copy(b, frm).wait_recv()
+                rs_copy(c, to).start()
+
+    def finish_step(j, c, frm, away, last):
+        done = jnp.logical_and(last, j % 2 == 1)
+
+        @pl.when(jnp.logical_and(valid(j, away), done))
+        def _():
+            finish(c // 2)
+            ag_copy(c - 1, frm).start()
+            ag_copy(c, frm).start()
+            use(c // 2)
+
+    def gather_step(j, c, frm, to, away, last):
+        @pl.when(valid(j, away))
+        def _():
+            ag_copy(c, frm).wait_recv()
 
             @pl.when(jnp.logical_not(last))
             def _():
-                ag_copy(b, to).start()
-
-            use(b)
+                ag_copy(c, to).start()
+
+    def use_step(j, c, away):
+        @pl.when(jnp.logical_and(valid(j, away), j % 2 == 1))
+        def _():
+            use(c // 2)
 
     def transpose_block(b):
         masked_t[:, pl.ds(pl.multiple_of(b * BLK, BLK), BLK)] = masked[b].T
 
-    steps = 2 * (ni - 1) + h
+    steps = 2 * ni + 2 * h - 1
     first, end = z == 0, z == ni - 1
     inner_first, inner_end = z > 0, z < ni - 1
 
+    def low(j):
+        return jnp.clip(j, 0, 2 * h - 1)
+
+    def high(j):
+        return low(j) + 2 * h
+
     @pl.loop(1, steps)
     def _(t):
-        j = t - z
-        reduce_step(j, jnp.clip(j, 0, h - 1) + h, left, right, inner_first, end)
-        j = t - (ni - 1 - z)
-        reduce_step(j, jnp.clip(j, 0, h - 1), right, left, inner_end, first)
-        j = t - (ni - 1) - z
-        gather_step(j, jnp.clip(j, 0, h - 1), left, right, inner_first, end)
-        j = t - 2 * (ni - 1) + z
-        gather_step(j, jnp.clip(j, 0, h - 1) + h, right, left, inner_end, first)
+        jr = t - z
+        jl = t - (ni - 1 - z)
+        gl = t - ni - z
+        gr = t - ni - (ni - 1 - z)
+        reduce_step(jr, high(jr), left, right, inner_first, end)
+        reduce_step(jl, low(jl), right, left, inner_end, first)
+        gather_step(gl, low(gl), left, right, inner_first, end)
+        gather_step(gr, high(gr), right, left, inner_end, first)
+        finish_step(jr, high(jr), left, inner_first, end)
+        finish_step(jl, low(jl), right, inner_end, first)
+        use_step(gl, low(gl), inner_first)
+        use_step(gr, high(gr), inner_end)
 
         @pl.when(t - 1 < ub)
         def _():
@@ -323,17 +414,17 @@
     for d in range(1, nu):
         cc_copy(d).wait_send()
 
-    @pl.loop(0, h)
-    def _(b):
+    @pl.loop(0, 2 * h)
+    def _(c):
         @pl.when(z > 0)
         def _():
-            rs_copy(b, left).wait_send()
-            ag_copy(b + h, left).wait_send()
+            rs_copy(c, left).wait_send()
+            ag_copy(c + 2 * h, left).wait_send()
 
         @pl.when(z < ni - 1)
         def _():
-            rs_copy(b + h, right).wait_send()
-            ag_copy(b, right).wait_send()
+            rs_copy(c + 2 * h, right).wait_send()
+            ag_copy(c, right).wait_send()
 
 
 def solution(mesh):
@@ -345,25 +436,31 @@
         ub, ib = users // BLK, items // BLK
         levels = nu.bit_length() - 1
         ibp = -(-ib // 8) * 8
+        sub = -(-(BLK + k // 2 + 8) // 16) * 8
         vm = pl.BlockSpec(memory_space=pltpu.VMEM)
-        sm = pl.BlockSpec(memory_space=pltpu.SMEM)
+        hbm = pl.BlockSpec(memory_space=pltpu.HBM)
         dma = pltpu.SemaphoreType.DMA
         new_users, new_items = pl.pallas_call(
             functools.partial(kernel, nu, ni),
             out_shape=(
-                jax.ShapeDtypeStruct((ub, BLK, k), f32),
+                jax.ShapeDtypeStruct((2 * ub, BLK // 2, k), f32),
                 jax.ShapeDtypeStruct((items, k), f32),
             ),
-            in_specs=[vm, sm, vm, vm, sm],
+            in_specs=[hbm] * 5,
             out_specs=(vm, vm),
             scratch_shapes=[
+                pltpu.VMEM((ub, BLK, items), bf16),
+                pltpu.SMEM((ub, ib), jnp.int32),
+                pltpu.VMEM((ub, BLK, k), f32),
+                pltpu.VMEM((items, k), f32),
+                pltpu.SMEM((2,), f32),
                 pltpu.VMEM((items, 2 * k), bf16),
                 pltpu.VMEM((ib, k, k), f32),
                 pltpu.VMEM((ub, BLK, items), bf16),
                 pltpu.VMEM((items, users), bf16),
                 pltpu.VMEM((8, items), f32),
-                pltpu.VMEM((ub, BLK + k + 8, k), f32),
-                pltpu.VMEM((ub, BLK + k + 8, k), f32),
+                pltpu.VMEM((2 * ub, sub, k), f32),
+                pltpu.VMEM((2 * ub, sub, k), f32),
                 pltpu.VMEM((users, 2 * k), bf16),
                 pltpu.VMEM((ib, k, k), f32),
                 pltpu.VMEM((items, k), f32),
@@ -373,10 +470,12 @@
             ]
             + [pltpu.VMEM((items >> (i + 1), k), f32) for i in range(levels)]
             + [
+                dma((4,)),
                 dma((ub,)),
-                dma((ub,)),
-                dma((ub,)),
-                dma((ub,)),
+                dma((2 * ub,)),
+                dma((2 * ub,)),
+                dma((2 * ub,)),
+                dma((2 * ub,)),
                 dma((nu - 1,)),
                 dma((nu - 1,)),
                 dma((levels,)),
@@ -385,7 +484,7 @@
                 dma((levels,)),
             ],
             compiler_params=pltpu.CompilerParams(
-                collective_id=0, has_side_effects=True, vmem_limit_bytes=40 * 2**20
+                collective_id=0, has_side_effects=True, vmem_limit_bytes=56 * 2**20
             ),
             cost_estimate=pl.CostEstimate(
                 flops=8 * users * items * k, bytes_accessed=2 * users * items, transcendentals=0

time: 67.5 us -> 70.1 us (1.039); the launches traced: 66.4 us -> 69.9 us
  Pallas kernels: 59 us -> 65.4 us
  local copies, waits for them, and re-layouts: 6.75 us -> 3.83 us
    pallas_call x1, Pallas kernels: 59 us -> 65.4 us  [body(): pl.pallas_call(functools.partial(kernel, nu, ni), out_shape=(jax.ShapeDty...]
    unnamed x12 -> x2, local copies, waits for them, and re-layouts: 6.75 us -> 3.83 us
where the time goes in v2:
time: 70.1 us; the launch traced here: 69.9 us
  Pallas kernels  65.4 us (93%)
  local copies, waits for them, and re-layouts  3.83 us (5%)
    pallas_call x1, Pallas kernels, body(): pl.pallas_call(functools.partial(kernel, nu, ni), out_shape=(jax.ShapeDty...  65.4 us
    unnamed x2, local copies, waits for them, and re-layouts  3.83 us

profile of v2, /device:TPU:0, one launch (start us, length us, event | category | flops | bytes accessed | tf_op | source)
XLA Modules:
  0.0 69.9 jit_solution(439596170035209671)
XLA Ops:
  0.6 65.4 %shard_map.68 = (f32[12,64,128]{2,1,0:T(8,128)}, f32[1536,128]{1,0:T(8,128)}) custom-call(bf16[768,1536]{1,0:T(8,128)(2,1)} %r_hbm.1, s32[6,12]{1,0:T(8,128)} %p_hbm.1, f32[6,128,128]{2,1,0:T(8,128)} %bitcast.3, f32[1536,128]{1,0:T(8,128)} %q_hbm.1, f32[2]{0:T(128)} %step_hbm.1), custom_call_target="tpu_custom_call" | custom-call | flops 1207959552 | bytes 2359296 | tf_op jit(solution)/shard_map/pallas_call | solution.py:443
  66.1 1.8 %copy.9 = f32[768,128]{1,0:T(8,128)} copy(f32[768,128]{1,0:T(8,128)} %bitcast.2) | data formatting | bytes 786432
  67.8 2.1 %copy.10 = f32[1536,128]{1,0:T(8,128)} copy(f32[1536,128]{1,0:T(8,128)} %get-tuple-element.9) | data formatting | bytes 1572864

commit v3 on v2

--- a/solution.py
+++ b/solution.py
@@ -28,18 +28,17 @@
     return x[:, :k] + x[:, k:]
 
 
-def dot3(x, y):
-    xh, xl = split(x)
-    yh, yl = split(y)
-    return jnp.dot(
-        jnp.concatenate([xh, xl, xh], axis=1),
-        jnp.concatenate([yh, yh, yl], axis=0),
-        preferred_element_type=f32,
-    )
-
-
-def gram(pair):
-    full = lax.dot_general(pair, pair, (((0,), (0,)), ((), ())), preferred_element_type=f32)
+def three(x):
+    hi, lo = split(x)
+    return jnp.concatenate([hi, hi, lo], axis=0)
+
+
+def stacked(x):
+    return jnp.concatenate(split(x.T), axis=0)
+
+
+def gram(stack, pair):
+    full = jnp.dot(stack, pair, preferred_element_type=f32)
     k = full.shape[0] // 2
     full = full[:k] + full[k:]
     return full[:, :k] + full[:, k:]
@@ -90,11 +89,10 @@
     qq,
     qg,
     masked,
-    masked_t,
     mask_row,
     part,
     rs_in,
-    pp,
+    ppt,
     hs,
     acc,
     scale,
@@ -185,13 +183,14 @@
     for copy in inputs:
         copy.wait()
 
-    @pl.loop(0, ib)
-    def _(i):
-        rows = pl.ds(pl.multiple_of(i * BLK, BLK), BLK)
-        pair = both(q_ref[rows, :])
+    for i in range(ib):
+        rows = pl.ds(i * BLK, BLK)
+        own = q_ref[rows, :]
+        pair = both(own)
         qq[rows, :] = pair
-        qg[i] = gram(pair)
-        hs[i] = jnp.zeros((k, k), f32)
+        qg[i] = gram(stacked(own), pair)
+    hs[...] = jnp.zeros_like(hs)
+    for i in range(ib):
         count = p_ref[0, i]
         for b in range(1, ub):
             count = count + p_ref[b, i]
@@ -199,37 +198,45 @@
 
     pl.semaphore_wait(barrier, nu - 1 + jnp.minimum(z, 1) + jnp.minimum(ni - 1 - z, 1))
 
-    @pl.loop(0, ub)
+    @pl.loop(0, 2)
     def _(m):
-        b = ordered(m)
-        total = p_ref[b, 0]
-        grams = jnp.zeros((k, k), f32)
-        for i in range(ib):
-            present = p_ref[b, i].astype(f32)
-            mask_row[:, i * BLK : (i + 1) * BLK] = jnp.full((8, BLK), present, f32)
-            grams = grams + present * qg[i]
-            if i:
-                total = total + p_ref[b, i]
-        fetch(b).wait()
-        kept = r_ref[b] * mask_row[0:1, :].astype(bf16)
-        masked[b] = kept
-        a = fold(jnp.dot(kept, qq[...], preferred_element_type=f32))
-        packed, diagonal = pack(grams)
-        part[2 * b, 0:kh] = packed
-        part[2 * b, kh : kh + 1] = diagonal
-        part[2 * b, kh + 1 : kh + 8] = jnp.full((7, k), total.astype(f32), f32)
-        part[2 * b, kh + 8 : sub] = a[:cut]
-        part[2 * b + 1, 0 : BLK - cut] = a[cut:]
-
-        @pl.when(jnp.logical_and(z == ni - 1, b < h))
-        def _():
-            rs_copy(2 * b, left).start()
-            rs_copy(2 * b + 1, left).start()
-
-        @pl.when(jnp.logical_and(z == 0, b >= h))
-        def _():
-            rs_copy(2 * b, right).start()
-            rs_copy(2 * b + 1, right).start()
+        base = lax.rem(m + 1 - late, 2) * h
+        for n in range(h):
+            b = base + n
+            total = p_ref[b, 0]
+            grams = jnp.zeros((k, k), f32)
+            for i in range(ib):
+                present = p_ref[b, i].astype(f32)
+                mask_row[n : n + 1, i * BLK : (i + 1) * BLK] = jnp.full((1, BLK), present, f32)
+                grams = grams + present * qg[i]
+                if i:
+                    total = total + p_ref[b, i]
+            packed, diagonal = pack(grams)
+            part[2 * b, 0:kh] = packed
+            part[2 * b, kh : kh + 1] = diagonal
+            part[2 * b, kh + 1 : kh + 8] = jnp.full((7, k), total.astype(f32), f32)
+        for n in range(h):
+            fetch(base + n).wait()
+        for n in range(h):
+            b = base + n
+            rows = pl.ds(pl.multiple_of(b * BLK, BLK), BLK)
+            masked[rows, :] = r_ref[b] * mask_row[n : n + 1, :].astype(bf16)
+        rows = pl.ds(pl.multiple_of(base * BLK, BLK), h * BLK)
+        a = fold(jnp.dot(masked[rows, :], qq[...], preferred_element_type=f32))
+        for n in range(h):
+            b = base + n
+            part[2 * b, kh + 8 : sub] = a[n * BLK : n * BLK + cut]
+            part[2 * b + 1, 0 : BLK - cut] = a[n * BLK + cut : (n + 1) * BLK]
+
+        @pl.when(jnp.logical_and(z == ni - 1, base == 0))
+        def _():
+            for n in range(2 * h):
+                rs_copy(2 * base + n, left).start()
+
+        @pl.when(jnp.logical_and(z == 0, base == h))
+        def _():
+            for n in range(2 * h):
+                rs_copy(2 * base + n, right).start()
 
     for d in range(1, nu):
         cc_copy(d).start()
@@ -237,8 +244,7 @@
     def finish(b):
         a = jnp.concatenate([part[2 * b, kh + 8 : sub], part[2 * b + 1, 0 : BLK - cut]], axis=0)
         g = unpack(part[2 * b, 0:kh], part[2 * b, kh : kh + 1])
-        gh, gl = split(g)
-        gs = jnp.concatenate([gh, gh, gl], axis=0)
+        gs = three(g)
         s = step_ref[0] / (BLK * (1.0 + part[2 * b, kh + 1 : kh + 2]))
         p = u_ref[b]
         for _ in range(2):
@@ -249,9 +255,10 @@
         ou_ref[2 * b + 1] = p[half:]
 
     def use(b):
-        pair = both(jnp.concatenate([ou_ref[2 * b], ou_ref[2 * b + 1]], axis=0))
-        pp[pl.ds(pl.multiple_of(b * BLK, BLK), BLK), :] = pair
-        g = gram(pair)
+        own = jnp.concatenate([ou_ref[2 * b], ou_ref[2 * b + 1]], axis=0)
+        stack = stacked(own)
+        ppt[:, pl.ds(pl.multiple_of(b * BLK, BLK), BLK)] = stack
+        g = gram(stack, both(own))
         for i in range(ib):
             hs[i] = hs[i] + p_ref[b, i].astype(f32) * g
 
@@ -291,9 +298,6 @@
         @pl.when(jnp.logical_and(valid(j, away), j % 2 == 1))
         def _():
             use(c // 2)
-
-    def transpose_block(b):
-        masked_t[:, pl.ds(pl.multiple_of(b * BLK, BLK), BLK)] = masked[b].T
 
     steps = 2 * ni + 2 * h - 1
     first, end = z == 0, z == ni - 1
@@ -313,19 +317,12 @@
         gr = t - ni - (ni - 1 - z)
         reduce_step(jr, high(jr), left, right, inner_first, end)
         reduce_step(jl, low(jl), right, left, inner_end, first)
+        finish_step(jr, high(jr), left, inner_first, end)
+        finish_step(jl, low(jl), right, inner_end, first)
         gather_step(gl, low(gl), left, right, inner_first, end)
         gather_step(gr, high(gr), right, left, inner_end, first)
-        finish_step(jr, high(jr), left, inner_first, end)
-        finish_step(jl, low(jl), right, inner_end, first)
         use_step(gl, low(gl), inner_first)
         use_step(gr, high(gr), inner_end)
-
-        @pl.when(t - 1 < ub)
-        def _():
-            transpose_block(jnp.minimum(t - 1, ub - 1))
-
-    for b in range(steps - 1, ub):
-        transpose_block(b)
 
     bits = [(u // (1 << i)) % 2 for i in range(levels)]
     partners = [u + (1 << i) * (1 - 2 * bits[i]) for i in range(levels)]
@@ -371,12 +368,15 @@
         )
 
     def product(base, n):
-        rows = pl.ds(pl.multiple_of(base, BLK), n)
-        acc[rows, :] = fold(jnp.dot(masked_t[rows, :], pp[...], preferred_element_type=f32))
+        base = pl.multiple_of(base, BLK)
+        wide = jnp.dot(ppt[...], masked[:, pl.ds(base, n)], preferred_element_type=f32)
+        wide = wide[:k] + wide[k:]
         for m in range(n // BLK):
-            block = base // BLK + m
-            own = pl.ds(pl.multiple_of(base + m * BLK, BLK), BLK)
-            acc[own, :] = acc[own, :] - dot3(q_ref[own, :], hs[block])
+            rows = pl.ds(pl.multiple_of(base + m * BLK, BLK), BLK)
+            pair = qq[rows, :]
+            left_side = jnp.concatenate([pair, pair[:, :k]], axis=1)
+            known = jnp.dot(left_side, three(hs[base // BLK + m]), preferred_element_type=f32)
+            acc[rows, :] = wide[:, m * BLK : (m + 1) * BLK].T - known
 
     n, keep, send, _ = plan[0]
     product(send, n)
@@ -443,8 +443,8 @@
         new_users, new_items = pl.pallas_call(
             functools.partial(kernel, nu, ni),
             out_shape=(
-                jax.ShapeDtypeStruct((2 * ub, BLK // 2, k), f32),
-                jax.ShapeDtypeStruct((items, k), f32),
+                pltpu.VMEM((2 * ub, BLK // 2, k), f32),
+                pltpu.VMEM((items, k), f32),
             ),
             in_specs=[hbm] * 5,
             out_specs=(vm, vm),
@@ -456,12 +456,11 @@
                 pltpu.SMEM((2,), f32),
                 pltpu.VMEM((items, 2 * k), bf16),
                 pltpu.VMEM((ib, k, k), f32),
-                pltpu.VMEM((ub, BLK, items), bf16),
-                pltpu.VMEM((items, users), bf16),
-                pltpu.VMEM((8, items), f32),
+                pltpu.VMEM((users, items), bf16),
+                pltpu.VMEM((-(-ub // 16) * 8, items), f32),
                 pltpu.VMEM((2 * ub, sub, k), f32),
                 pltpu.VMEM((2 * ub, sub, k), f32),
-                pltpu.VMEM((users, 2 * k), bf16),
+                pltpu.VMEM((2 * k, users), bf16),
                 pltpu.VMEM((ib, k, k), f32),
                 pltpu.VMEM((items, k), f32),
                 pltpu.VMEM((items, k), f32),

time: 70.1 us -> 61.3 us (0.87)
  Pallas kernels: 65.4 us -> 58.9 us
  local copies, waits for them, and re-layouts: 3.83 us -> 1.63 us
    pallas_call x1, Pallas kernels: 65.4 us -> 58.9 us  [body(): pl.pallas_call(functools.partial(kernel, nu, ni), out_shape=(pltpu.VMEM((...]
    unnamed x2, local copies, waits for them, and re-layouts: 3.83 us -> 1.63 us
where the time goes in v3:
time: 61.3 us; the launch traced here: 61.2 us
  Pallas kernels  58.9 us (96%)
  local copies, waits for them, and re-layouts  1.63 us (3%)
  between operations  0.64 us (1%)
    pallas_call x1, Pallas kernels, body(): pl.pallas_call(functools.partial(kernel, nu, ni), out_shape=(pltpu.VMEM((...  58.9 us
    unnamed x2, local copies, waits for them, and re-layouts  1.63 us

profile of v3, /device:TPU:0, one launch (start us, length us, event | category | flops | bytes accessed | tf_op | source)
XLA Modules:
  0.0 61.2 jit_solution(346668994002923275)
XLA Ops:
  0.6 58.9 %shard_map.68 = (f32[12,64,128]{2,1,0:T(8,128)S(1)}, f32[1536,128]{1,0:T(8,128)S(1)}) custom-call(bf16[768,1536]{1,0:T(8,128)(2,1)} %r_hbm.1, s32[6,12]{1,0:T(8,128)} %p_hbm.1, f32[6,128,128]{2,1,0:T(8,128)} %bitcast.3, f32[1536,128]{1,0:T(8,128)} %q_hbm.1, f32[2]{0:T(128)} %step_hbm.1), custom_call_target="tpu_custom_call" | custom-call | flops 1207959552 | bytes 2359296 | tf_op jit(solution)/shard_map/pallas_call | solution.py:443
  59.5 0.7 %copy.9 = f32[768,128]{1,0:T(8,128)} copy(f32[768,128]{1,0:T(8,128)S(1)} %bitcast.2) | data formatting | bytes 786432
  60.3 0.9 %copy.10 = f32[1536,128]{1,0:T(8,128)} copy(f32[1536,128]{1,0:T(8,128)S(1)} %get-tuple-element.7) | data formatting | bytes 1572864

commit v4 on v3

--- a/solution.py
+++ b/solution.py
@@ -1,4 +1,5 @@
 import functools
+import itertools
 
 import jax
 import jax.numpy as jnp
@@ -8,6 +9,7 @@
 from jax.sharding import PartitionSpec as P
 
 BLK = 128
+LAG = 3
 f32 = jnp.float32
 bf16 = jnp.bfloat16
 MESH = pl.DeviceIdType.MESH
@@ -98,11 +100,11 @@
     scale,
     cc_out,
     cc_in,
+    halves,
     *rest,
 ):
     levels = nu.bit_length() - 1
-    halves = rest[:levels]
-    (in_s, row_s, rs_s, rs_r, ag_s, ag_r, cc_s, cc_r, hv_s, hv_r, db_s, db_r) = rest[levels:]
+    (in_s, row_s, rs_s, rs_r, ag_s, ag_r, cc_s, cc_r, hv_s, hv_r, db_s, db_r) = rest
     ub, _, k = u_ref.shape
     items = q_ref.shape[0]
     ib = items // BLK
@@ -299,7 +301,7 @@
         def _():
             use(c // 2)
 
-    steps = 2 * ni + 2 * h - 1
+    far = LAG * (ni - 1)
     first, end = z == 0, z == ni - 1
     inner_first, inner_end = z > 0, z < ni - 1
 
@@ -309,12 +311,12 @@
     def high(j):
         return low(j) + 2 * h
 
-    @pl.loop(1, steps)
+    @pl.loop(LAG, 2 * far + 2 * h + 1)
     def _(t):
-        jr = t - z
-        jl = t - (ni - 1 - z)
-        gl = t - ni - z
-        gr = t - ni - (ni - 1 - z)
+        jr = t - LAG * z
+        jl = t - (far - LAG * z)
+        gl = t - far - 1 - LAG * z
+        gr = t - far - 1 - (far - LAG * z)
         reduce_step(jr, high(jr), left, right, inner_first, end)
         reduce_step(jl, low(jl), right, left, inner_end, first)
         finish_step(jr, high(jr), left, inner_first, end)
@@ -328,42 +330,64 @@
     partners = [u + (1 << i) * (1 - 2 * bits[i]) for i in range(levels)]
     core = bits[0]
 
-    def pick(xs, level):
+    def pick(xs, level, which):
         if level == 0:
             return xs[0]
         one, two = xs[level], xs[levels - level]
-        return one + core * (two - one)
-
-    size = items
-    start = 0
-    plan = []
-    for level in range(levels):
-        size = size // 2
-        bit = pick(bits, level)
-        keep = pl.multiple_of(start + bit * size, 8)
-        send = pl.multiple_of(start + (1 - bit) * size, 8)
-        plan.append((size, keep, send, pick(partners, level)))
-        start = keep
-
-    def half_copy(level):
-        n, _, send, to = plan[level]
+        return one + which * (two - one)
+
+    mine = [pick(bits, n, core) for n in range(levels)]
+    theirs = [pick(bits, n, 1 - core) for n in range(levels)]
+    to = [pick(partners, n, core) for n in range(levels)]
+    leaf = items >> levels
+    offset = [sum(1 << (levels - m - 1) for m in range(n)) for n in range(levels)]
+
+    def tails(level):
+        return list(itertools.product((0, 1), repeat=levels - level - 1))
+
+    def place(level, tail):
+        number = 0
+        for f in tail:
+            number = 2 * number + f
+        return offset[level] + number
+
+    def rows_of(digits):
+        start = 0
+        for n, d in enumerate(digits):
+            start = start + d * (items >> (n + 1))
+        return pl.ds(pl.multiple_of(start, 8), leaf)
+
+    def turned(known, tail):
+        ahead = known[levels - len(tail) :] if tail else []
+        return [1 - d if f else d for d, f in zip(ahead, tail)]
+
+    def sent(level, tail):
+        known = mine if level else theirs
+        return rows_of(mine[:level] + [1 - mine[level]] + turned(known, tail))
+
+    def held(level, tail):
+        return rows_of(mine[: level + 1] + turned(mine, tail))
+
+    def half_copy(level, tail):
+        n = place(level, tail)
         return pltpu.make_async_remote_copy(
-            src_ref=acc.at[pl.ds(send, n)],
-            dst_ref=halves[level],
-            send_sem=hv_s.at[level],
-            recv_sem=hv_r.at[level],
-            device_id=(to, z),
+            src_ref=acc.at[sent(level, tail)],
+            dst_ref=halves.at[n],
+            send_sem=hv_s.at[n],
+            recv_sem=hv_r.at[n],
+            device_id=(to[level], z),
             device_id_type=MESH,
         )
 
-    def double_copy(level):
-        n, keep, _, to = plan[level]
+    def double_copy(level, tail):
+        n = place(level, tail)
+        rows = held(level, tail)
         return pltpu.make_async_remote_copy(
-            src_ref=oi_ref.at[pl.ds(keep, n)],
-            dst_ref=oi_ref.at[pl.ds(keep, n)],
-            send_sem=db_s.at[level],
-            recv_sem=db_r.at[level],
-            device_id=(to, z),
+            src_ref=oi_ref.at[rows],
+            dst_ref=oi_ref.at[rows],
+            send_sem=db_s.at[n],
+            recv_sem=db_r.at[n],
+            device_id=(to[level], z),
             device_id_type=MESH,
         )
 
@@ -378,10 +402,16 @@
             known = jnp.dot(left_side, three(hs[base // BLK + m]), preferred_element_type=f32)
             acc[rows, :] = wide[:, m * BLK : (m + 1) * BLK].T - known
 
-    n, keep, send, _ = plan[0]
-    product(send, n)
-    half_copy(0).start()
-    product(keep, n)
+    quarter = items // 4
+    for f in (1, 0):
+        second = 1 - theirs[1] if f else theirs[1]
+        product((1 - mine[0]) * 2 * quarter + second * quarter, quarter)
+        for tail in reversed(tails(0)):
+            if tail[0] == f:
+                half_copy(0, tail).start()
+    for f in (1, 0):
+        second = 1 - mine[1] if f else mine[1]
+        product(mine[0] * 2 * quarter + second * quarter, quarter)
 
     for d in range(1, nu):
         cc_copy(d).wait_recv()
@@ -393,24 +423,30 @@
         scale[i * BLK : (i + 1) * BLK, :] = jnp.broadcast_to(scaling[i : i + 1], (BLK, k))
 
     for level in range(levels):
-        n, keep, _, _ = plan[level]
-        if level:
-            half_copy(level).start()
-        half_copy(level).wait_recv()
-        rows = pl.ds(keep, n)
-        if level < levels - 1:
-            acc[rows, :] = acc[rows, :] + halves[level][...]
-        else:
-            oi_ref[rows, :] = q_ref[rows, :] + (acc[rows, :] + halves[level][...]) * scale[rows, :]
+        for tail in reversed(tails(level)):
+            half_copy(level, tail).wait_recv()
+            rows = held(level, tail)
+            summed = acc[rows, :] + halves[place(level, tail)]
+            if tail:
+                acc[rows, :] = summed
+                if tail[0]:
+                    half_copy(level + 1, tail[1:]).start()
+            else:
+                oi_ref[rows, :] = q_ref[rows, :] + summed * scale[rows, :]
 
     for level in reversed(range(levels)):
-        double_copy(level).start()
-        n, keep, send, to = plan[level]
-        double_copy(level).wait_recv()
+        double_copy(level, (0,) * (levels - level - 1)).start()
+    for level in reversed(range(levels)):
+        for tail in tails(level):
+            double_copy(level, tail).wait_recv()
+            for lower in reversed(range(level)):
+                middle = (0,) * (level - lower - 1)
+                double_copy(lower, middle + (1,) + tail).start()
 
     for level in range(levels):
-        half_copy(level).wait_send()
-        double_copy(level).wait_send()
+        for tail in tails(level):
+            half_copy(level, tail).wait_send()
+            double_copy(level, tail).wait_send()
     for d in range(1, nu):
         cc_copy(d).wait_send()
 
@@ -434,7 +470,6 @@
         users, items = ratings.shape
         k = item_factors.shape[1]
         ub, ib = users // BLK, items // BLK
-        levels = nu.bit_length() - 1
         ibp = -(-ib // 8) * 8
         sub = -(-(BLK + k // 2 + 8) // 16) * 8
         vm = pl.BlockSpec(memory_space=pltpu.VMEM)
@@ -466,9 +501,7 @@
                 pltpu.VMEM((items, k), f32),
                 pltpu.VMEM((ibp, k), f32),
                 pltpu.VMEM((nu - 1, ibp, k), f32),
-            ]
-            + [pltpu.VMEM((items >> (i + 1), k), f32) for i in range(levels)]
-            + [
+                pltpu.VMEM((nu - 1, items // nu, k), f32),
                 dma((4,)),
                 dma((ub,)),
                 dma((2 * ub,)),
@@ -477,10 +510,10 @@
                 dma((2 * ub,)),
                 dma((nu - 1,)),
                 dma((nu - 1,)),
-                dma((levels,)),
-                dma((levels,)),
-                dma((levels,)),
-                dma((levels,)),
+                dma((nu - 1,)),
+                dma((nu - 1,)),
+                dma((nu - 1,)),
+                dma((nu - 1,)),
             ],
             compiler_params=pltpu.CompilerParams(
                 collective_id=0, has_side_effects=True, vmem_limit_bytes=56 * 2**20

time: 61.3 us -> 53.2 us (0.87)
  Pallas kernels: 58.9 us -> 50.8 us
    pallas_call x1, Pallas kernels: 58.9 us -> 50.8 us  [body(): pl.pallas_call(functools.partial(kernel, nu, ni), out_shape=(pltpu.VMEM((...]
where the time goes in v4:
time: 53.2 us; the launch traced here: 53.1 us
  Pallas kernels  50.8 us (95%)
  local copies, waits for them, and re-layouts  1.63 us (3%)
  between operations  0.64 us (1%)
    pallas_call x1, Pallas kernels, body(): pl.pallas_call(functools.partial(kernel, nu, ni), out_shape=(pltpu.VMEM((...  50.8 us
    unnamed x2, local copies, waits for them, and re-layouts  1.63 us

profile of v4, /device:TPU:0, one launch (start us, length us, event | category | flops | bytes accessed | tf_op | source)
XLA Modules:
  0.0 53.1 jit_solution(3910200014699364827)
XLA Ops:
  0.6 50.8 %shard_map.68 = (f32[12,64,128]{2,1,0:T(8,128)S(1)}, f32[1536,128]{1,0:T(8,128)S(1)}) custom-call(bf16[768,1536]{1,0:T(8,128)(2,1)} %r_hbm.1, s32[6,12]{1,0:T(8,128)} %p_hbm.1, f32[6,128,128]{2,1,0:T(8,128)} %bitcast.3, f32[1536,128]{1,0:T(8,128)} %q_hbm.1, f32[2]{0:T(128)} %step_hbm.1), custom_call_target="tpu_custom_call" | custom-call | flops 1207959552 | bytes 2359296 | tf_op jit(solution)/shard_map/pallas_call | solution.py:478
  51.4 0.7 %copy.9 = f32[768,128]{1,0:T(8,128)} copy(f32[768,128]{1,0:T(8,128)S(1)} %bitcast.2) | data formatting | bytes 786432
  52.2 0.9 %copy.10 = f32[1536,128]{1,0:T(8,128)} copy(f32[1536,128]{1,0:T(8,128)S(1)} %get-tuple-element.7) | data formatting | bytes 1572864

commit v5 on v4

--- a/solution.py
+++ b/solution.py
@@ -92,8 +92,12 @@
     qg,
     masked,
     mask_row,
-    part,
-    rs_in,
+    gpart,
+    g_in,
+    apart,
+    a_in,
+    g_three,
+    g_scale,
     ppt,
     hs,
     acc,
@@ -104,15 +108,13 @@
     *rest,
 ):
     levels = nu.bit_length() - 1
-    (in_s, row_s, rs_s, rs_r, ag_s, ag_r, cc_s, cc_r, hv_s, hv_r, db_s, db_r) = rest
-    ub, _, k = u_ref.shape
+    (in_s, row_s, gs_s, gs_r, rs_s, rs_r, ag_s, ag_r, cc_s, cc_r, hv_s, hv_r, db_s, db_r) = rest
+    ub, k = gpart.shape[0], gpart.shape[2]
     items = q_ref.shape[0]
     ib = items // BLK
     h = ub // 2
     half = BLK // 2
     kh = k // 2
-    sub = part.shape[1]
-    cut = sub - kh - 8
     u = lax.axis_index("user")
     z = lax.axis_index("item")
 
@@ -149,12 +151,22 @@
     def _():
         pl.semaphore_signal(barrier, inc=1, device_id=(u, z + 1), device_id_type=MESH)
 
-    def rs_copy(b, to):
+    def g_copy(b, to):
         return pltpu.make_async_remote_copy(
-            src_ref=part.at[b],
-            dst_ref=rs_in.at[b],
-            send_sem=rs_s.at[b],
-            recv_sem=rs_r.at[b],
+            src_ref=gpart.at[b],
+            dst_ref=g_in.at[b],
+            send_sem=gs_s.at[b],
+            recv_sem=gs_r.at[b],
+            device_id=(u, to),
+            device_id_type=MESH,
+        )
+
+    def a_copy(c, to):
+        return pltpu.make_async_remote_copy(
+            src_ref=apart.at[c],
+            dst_ref=a_in.at[c],
+            send_sem=rs_s.at[c],
+            recv_sem=rs_r.at[c],
             device_id=(u, to),
             device_id_type=MESH,
         )
@@ -214,9 +226,20 @@
                 if i:
                     total = total + p_ref[b, i]
             packed, diagonal = pack(grams)
-            part[2 * b, 0:kh] = packed
-            part[2 * b, kh : kh + 1] = diagonal
-            part[2 * b, kh + 1 : kh + 8] = jnp.full((7, k), total.astype(f32), f32)
+            gpart[b, 0:kh] = packed
+            gpart[b, kh : kh + 1] = diagonal
+            gpart[b, kh + 1 : kh + 8] = jnp.full((7, k), total.astype(f32), f32)
+
+        @pl.when(jnp.logical_and(z == ni - 1, base == 0))
+        def _():
+            for n in range(h):
+                g_copy(base + n, left).start()
+
+        @pl.when(jnp.logical_and(z == 0, base == h))
+        def _():
+            for n in range(h):
+                g_copy(base + n, right).start()
+
         for n in range(h):
             fetch(base + n).wait()
         for n in range(h):
@@ -225,36 +248,37 @@
             masked[rows, :] = r_ref[b] * mask_row[n : n + 1, :].astype(bf16)
         rows = pl.ds(pl.multiple_of(base * BLK, BLK), h * BLK)
         a = fold(jnp.dot(masked[rows, :], qq[...], preferred_element_type=f32))
-        for n in range(h):
-            b = base + n
-            part[2 * b, kh + 8 : sub] = a[n * BLK : n * BLK + cut]
-            part[2 * b + 1, 0 : BLK - cut] = a[n * BLK + cut : (n + 1) * BLK]
+        for n in range(2 * h):
+            apart[2 * base + n] = a[n * half : (n + 1) * half]
 
         @pl.when(jnp.logical_and(z == ni - 1, base == 0))
         def _():
             for n in range(2 * h):
-                rs_copy(2 * base + n, left).start()
+                a_copy(2 * base + n, left).start()
 
         @pl.when(jnp.logical_and(z == 0, base == h))
         def _():
             for n in range(2 * h):
-                rs_copy(2 * base + n, right).start()
+                a_copy(2 * base + n, right).start()
 
     for d in range(1, nu):
         cc_copy(d).start()
 
-    def finish(b):
-        a = jnp.concatenate([part[2 * b, kh + 8 : sub], part[2 * b + 1, 0 : BLK - cut]], axis=0)
-        g = unpack(part[2 * b, 0:kh], part[2 * b, kh : kh + 1])
-        gs = three(g)
-        s = step_ref[0] / (BLK * (1.0 + part[2 * b, kh + 1 : kh + 2]))
-        p = u_ref[b]
+    def prepare(b):
+        g_three[b] = three(unpack(gpart[b, 0:kh], gpart[b, kh : kh + 1]))
+        counted = 1.0 + gpart[b, kh + 1 : kh + 2]
+        g_scale[b] = jnp.broadcast_to(step_ref[0] / (BLK * counted), (8, k))
+
+    def finish(c):
+        gs = g_three[c // 2]
+        s = g_scale[c // 2, 0:1]
+        a = apart[c]
+        p = u_ref[c]
         for _ in range(2):
             ph, pl_ = split(p)
             ps = jnp.concatenate([ph, pl_, ph], axis=1)
             p = p + s * (a - jnp.dot(ps, gs, preferred_element_type=f32))
-        ou_ref[2 * b] = p[:half]
-        ou_ref[2 * b + 1] = p[half:]
+        ou_ref[c] = p
 
     def use(b):
         own = jnp.concatenate([ou_ref[2 * b], ou_ref[2 * b + 1]], axis=0)
@@ -264,31 +288,44 @@
         for i in range(ib):
             hs[i] = hs[i] + p_ref[b, i].astype(f32) * g
 
-    def valid(j, away):
-        return jnp.logical_and(away, jnp.logical_and(j >= 0, j < 2 * h))
-
-    def reduce_step(j, c, frm, to, away, last):
-        @pl.when(valid(j, away))
-        def _():
-            rs_copy(c, frm).wait_recv()
-            part[c] = part[c] + rs_in[c]
+    def valid(j, away, count):
+        return jnp.logical_and(away, jnp.logical_and(j >= 0, j < count))
+
+    def g_step(j, b, frm, to, away, last):
+        @pl.when(valid(j, away, h))
+        def _():
+            g_copy(b, frm).wait_recv()
+            gpart[b] = gpart[b] + g_in[b]
 
             @pl.when(jnp.logical_not(last))
             def _():
-                rs_copy(c, to).start()
-
-    def finish_step(j, c, frm, away, last):
-        done = jnp.logical_and(last, j % 2 == 1)
-
-        @pl.when(jnp.logical_and(valid(j, away), done))
-        def _():
-            finish(c // 2)
-            ag_copy(c - 1, frm).start()
-            ag_copy(c, frm).start()
-            use(c // 2)
+                g_copy(b, to).start()
+
+            @pl.when(last)
+            def _():
+                prepare(b)
+
+    def a_step(j, c, frm, to, away, last):
+        @pl.when(valid(j, away, 2 * h))
+        def _():
+            a_copy(c, frm).wait_recv()
+            apart[c] = apart[c] + a_in[c]
+
+            @pl.when(jnp.logical_not(last))
+            def _():
+                a_copy(c, to).start()
+
+            @pl.when(last)
+            def _():
+                finish(c)
+                ag_copy(c, frm).start()
+
+            @pl.when(jnp.logical_and(last, j % 2 == 1))
+            def _():
+                use(c // 2)
 
     def gather_step(j, c, frm, to, away, last):
-        @pl.when(valid(j, away))
+        @pl.when(valid(j, away, 2 * h))
         def _():
             ag_copy(c, frm).wait_recv()
 
@@ -297,7 +334,7 @@
                 ag_copy(c, to).start()
 
     def use_step(j, c, away):
-        @pl.when(jnp.logical_and(valid(j, away), j % 2 == 1))
+        @pl.when(jnp.logical_and(valid(j, away, 2 * h), j % 2 == 1))
         def _():
             use(c // 2)
 
@@ -305,22 +342,25 @@
     first, end = z == 0, z == ni - 1
     inner_first, inner_end = z > 0, z < ni - 1
 
+    def block(j):
+        return jnp.clip(j, 0, h - 1)
+
     def low(j):
         return jnp.clip(j, 0, 2 * h - 1)
 
     def high(j):
         return low(j) + 2 * h
 
-    @pl.loop(LAG, 2 * far + 2 * h + 1)
+    @pl.loop(LAG, 2 * far + 3 * h)
     def _(t):
         jr = t - LAG * z
         jl = t - (far - LAG * z)
-        gl = t - far - 1 - LAG * z
-        gr = t - far - 1 - (far - LAG * z)
-        reduce_step(jr, high(jr), left, right, inner_first, end)
-        reduce_step(jl, low(jl), right, left, inner_end, first)
-        finish_step(jr, high(jr), left, inner_first, end)
-        finish_step(jl, low(jl), right, inner_end, first)
+        gl = t - far - h - LAG * z
+        gr = t - far - h - (far - LAG * z)
+        g_step(jr, block(jr) + h, left, right, inner_first, end)
+        g_step(jl, block(jl), right, left, inner_end, first)
+        a_step(jr - h, high(jr - h), left, right, inner_first, end)
+        a_step(jl - h, low(jl - h), right, left, inner_end, first)
         gather_step(gl, low(gl), left, right, inner_first, end)
         gather_step(gr, high(gr), right, left, inner_end, first)
         use_step(gl, low(gl), inner_first)
@@ -454,13 +494,23 @@
     def _(c):
         @pl.when(z > 0)
         def _():
-            rs_copy(c, left).wait_send()
+            a_copy(c, left).wait_send()
             ag_copy(c + 2 * h, left).wait_send()
 
         @pl.when(z < ni - 1)
         def _():
-            rs_copy(c + 2 * h, right).wait_send()
+            a_copy(c + 2 * h, right).wait_send()
             ag_copy(c, right).wait_send()
+
+    @pl.loop(0, h)
+    def _(b):
+        @pl.when(z > 0)
+        def _():
+            g_copy(b, left).wait_send()
+
+        @pl.when(z < ni - 1)
+        def _():
+            g_copy(b + h, right).wait_send()
 
 
 def solution(mesh):
@@ -471,7 +521,6 @@
         k = item_factors.shape[1]
         ub, ib = users // BLK, items // BLK
         ibp = -(-ib // 8) * 8
-        sub = -(-(BLK + k // 2 + 8) // 16) * 8
         vm = pl.BlockSpec(memory_space=pltpu.VMEM)
         hbm = pl.BlockSpec(memory_space=pltpu.HBM)
         dma = pltpu.SemaphoreType.DMA
@@ -486,15 +535,19 @@
             scratch_shapes=[
                 pltpu.VMEM((ub, BLK, items), bf16),
                 pltpu.SMEM((ub, ib), jnp.int32),
-                pltpu.VMEM((ub, BLK, k), f32),
+                pltpu.VMEM((2 * ub, BLK // 2, k), f32),
                 pltpu.VMEM((items, k), f32),
                 pltpu.SMEM((2,), f32),
                 pltpu.VMEM((items, 2 * k), bf16),
                 pltpu.VMEM((ib, k, k), f32),
                 pltpu.VMEM((users, items), bf16),
                 pltpu.VMEM((-(-ub // 16) * 8, items), f32),
-                pltpu.VMEM((2 * ub, sub, k), f32),
-                pltpu.VMEM((2 * ub, sub, k), f32),
+                pltpu.VMEM((ub, k // 2 + 8, k), f32),
+                pltpu.VMEM((ub, k // 2 + 8, k), f32),
+                pltpu.VMEM((2 * ub, BLK // 2, k), f32),
+                pltpu.VMEM((2 * ub, BLK // 2, k), f32),
+                pltpu.VMEM((ub, 3 * k, k), bf16),
+                pltpu.VMEM((ub, 8, k), f32),
                 pltpu.VMEM((2 * k, users), bf16),
                 pltpu.VMEM((ib, k, k), f32),
                 pltpu.VMEM((items, k), f32),
@@ -503,6 +556,8 @@
                 pltpu.VMEM((nu - 1, ibp, k), f32),
                 pltpu.VMEM((nu - 1, items // nu, k), f32),
                 dma((4,)),
+                dma((ub,)),
+                dma((ub,)),
                 dma((ub,)),
                 dma((2 * ub,)),
                 dma((2 * ub,)),
@@ -521,7 +576,7 @@
             cost_estimate=pl.CostEstimate(
                 flops=8 * users * items * k, bytes_accessed=2 * users * items, transcendentals=0
             ),
-        )(ratings, presence, user_factors.reshape(ub, BLK, k), item_factors, step_sizes)
+        )(ratings, presence, user_factors.reshape(2 * ub, BLK // 2, k), item_factors, step_sizes)
         return new_users.reshape(users, k), new_items
 
     return jax.shard_map(

time: 53.2 us -> 52.3 us (0.983)
  Pallas kernels: 50.8 us -> 49.9 us
    pallas_call x1, Pallas kernels: 50.8 us -> 49.9 us  [body(): pl.pallas_call(functools.partial(kernel, nu, ni), out_shape=(pltpu.VMEM((...]
where the time goes in v5:
time: 52.3 us; the launch traced here: 52.2 us
  Pallas kernels  49.9 us (95%)
  local copies, waits for them, and re-layouts  1.63 us (3%)
  between operations  0.64 us (1%)
    pallas_call x1, Pallas kernels, body(): pl.pallas_call(functools.partial(kernel, nu, ni), out_shape=(pltpu.VMEM((...  49.9 us
    unnamed x2, local copies, waits for them, and re-layouts  1.63 us

profile of v5, /device:TPU:0, one launch (start us, length us, event | category | flops | bytes accessed | tf_op | source)
XLA Modules:
  0.0 52.2 jit_solution(500786701046561157)
XLA Ops:
  0.6 49.9 %shard_map.68 = (f32[12,64,128]{2,1,0:T(8,128)S(1)}, f32[1536,128]{1,0:T(8,128)S(1)}) custom-call(bf16[768,1536]{1,0:T(8,128)(2,1)} %r_hbm.1, s32[6,12]{1,0:T(8,128)} %p_hbm.1, f32[12,64,128]{2,1,0:T(8,128)} %bitcast.3, f32[1536,128]{1,0:T(8,128)} %q_hbm.1, f32[2]{0:T(128)} %step_hbm.1), custom_call_target="tpu_custom_call" | custom-call | flops 1207959552 | bytes 2359296 | tf_op jit(solution)/shard_map/pallas_call | solution.py:527
  50.5 0.7 %copy.9 = f32[768,128]{1,0:T(8,128)} copy(f32[768,128]{1,0:T(8,128)S(1)} %bitcast.2) | data formatting | bytes 786432
  51.3 0.9 %copy.10 = f32[1536,128]{1,0:T(8,128)} copy(f32[1536,128]{1,0:T(8,128)S(1)} %get-tuple-element.7) | data formatting | bytes 1572864

commit v6 on v5

--- a/solution.py
+++ b/solution.py
@@ -9,6 +9,7 @@
 from jax.sharding import PartitionSpec as P
 
 BLK = 128
+PIECES = 2
 LAG = 3
 f32 = jnp.float32
 bf16 = jnp.bfloat16
@@ -33,6 +34,11 @@
 def three(x):
     hi, lo = split(x)
     return jnp.concatenate([hi, hi, lo], axis=0)
+
+
+def times(x, y_three):
+    hi, lo = split(x)
+    return jnp.dot(jnp.concatenate([hi, lo, hi], axis=1), y_three, preferred_element_type=f32)
 
 
 def stacked(x):
@@ -98,6 +104,7 @@
     a_in,
     g_three,
     g_scale,
+    foreseen,
     ppt,
     hs,
     acc,
@@ -113,7 +120,8 @@
     items = q_ref.shape[0]
     ib = items // BLK
     h = ub // 2
-    half = BLK // 2
+    piece = BLK // PIECES
+    count = PIECES * h
     kh = k // 2
     u = lax.axis_index("user")
     z = lax.axis_index("item")
@@ -205,10 +213,10 @@
         qg[i] = gram(stacked(own), pair)
     hs[...] = jnp.zeros_like(hs)
     for i in range(ib):
-        count = p_ref[0, i]
+        present = p_ref[0, i]
         for b in range(1, ub):
-            count = count + p_ref[b, i]
-        cc_out[pl.ds(i, 1), :] = jnp.full((1, k), count.astype(f32), f32)
+            present = present + p_ref[b, i]
+        cc_out[pl.ds(i, 1), :] = jnp.full((1, k), present.astype(f32), f32)
 
     pl.semaphore_wait(barrier, nu - 1 + jnp.minimum(z, 1) + jnp.minimum(ni - 1 - z, 1))
 
@@ -248,18 +256,18 @@
             masked[rows, :] = r_ref[b] * mask_row[n : n + 1, :].astype(bf16)
         rows = pl.ds(pl.multiple_of(base * BLK, BLK), h * BLK)
         a = fold(jnp.dot(masked[rows, :], qq[...], preferred_element_type=f32))
-        for n in range(2 * h):
-            apart[2 * base + n] = a[n * half : (n + 1) * half]
+        for n in range(count):
+            apart[PIECES * base + n] = a[n * piece : (n + 1) * piece]
 
         @pl.when(jnp.logical_and(z == ni - 1, base == 0))
         def _():
-            for n in range(2 * h):
-                a_copy(2 * base + n, left).start()
+            for n in range(count):
+                a_copy(PIECES * base + n, left).start()
 
         @pl.when(jnp.logical_and(z == 0, base == h))
         def _():
-            for n in range(2 * h):
-                a_copy(2 * base + n, right).start()
+            for n in range(count):
+                a_copy(PIECES * base + n, right).start()
 
     for d in range(1, nu):
         cc_copy(d).start()
@@ -268,20 +276,19 @@
         g_three[b] = three(unpack(gpart[b, 0:kh], gpart[b, kh : kh + 1]))
         counted = 1.0 + gpart[b, kh + 1 : kh + 2]
         g_scale[b] = jnp.broadcast_to(step_ref[0] / (BLK * counted), (8, k))
+        p = jnp.concatenate([u_ref[PIECES * b + n] for n in range(PIECES)], axis=0)
+        known = times(p, g_three[b])
+        for n in range(PIECES):
+            foreseen[PIECES * b + n] = known[n * piece : (n + 1) * piece]
 
     def finish(c):
-        gs = g_three[c // 2]
-        s = g_scale[c // 2, 0:1]
-        a = apart[c]
-        p = u_ref[c]
-        for _ in range(2):
-            ph, pl_ = split(p)
-            ps = jnp.concatenate([ph, pl_, ph], axis=1)
-            p = p + s * (a - jnp.dot(ps, gs, preferred_element_type=f32))
-        ou_ref[c] = p
+        b = c // PIECES
+        s = g_scale[b, 0:1]
+        d = apart[c] - foreseen[c]
+        ou_ref[c] = u_ref[c] + s * (2.0 * d - s * times(d, g_three[b]))
 
     def use(b):
-        own = jnp.concatenate([ou_ref[2 * b], ou_ref[2 * b + 1]], axis=0)
+        own = jnp.concatenate([ou_ref[PIECES * b + n] for n in range(PIECES)], axis=0)
         stack = stacked(own)
         ppt[:, pl.ds(pl.multiple_of(b * BLK, BLK), BLK)] = stack
         g = gram(stack, both(own))
@@ -306,7 +313,7 @@
                 prepare(b)
 
     def a_step(j, c, frm, to, away, last):
-        @pl.when(valid(j, away, 2 * h))
+        @pl.when(valid(j, away, count))
         def _():
             a_copy(c, frm).wait_recv()
             apart[c] = apart[c] + a_in[c]
@@ -320,12 +327,8 @@
                 finish(c)
                 ag_copy(c, frm).start()
 
-            @pl.when(jnp.logical_and(last, j % 2 == 1))
-            def _():
-                use(c // 2)
-
     def gather_step(j, c, frm, to, away, last):
-        @pl.when(valid(j, away, 2 * h))
+        @pl.when(valid(j, away, count))
         def _():
             ag_copy(c, frm).wait_recv()
 
@@ -334,9 +337,9 @@
                 ag_copy(c, to).start()
 
     def use_step(j, c, away):
-        @pl.when(jnp.logical_and(valid(j, away, 2 * h), j % 2 == 1))
-        def _():
-            use(c // 2)
+        @pl.when(jnp.logical_and(valid(j, away, count), j % PIECES == PIECES - 1))
+        def _():
+            use(c // PIECES)
 
     far = LAG * (ni - 1)
     first, end = z == 0, z == ni - 1
@@ -346,12 +349,12 @@
         return jnp.clip(j, 0, h - 1)
 
     def low(j):
-        return jnp.clip(j, 0, 2 * h - 1)
+        return jnp.clip(j, 0, count - 1)
 
     def high(j):
-        return low(j) + 2 * h
-
-    @pl.loop(LAG, 2 * far + 3 * h)
+        return low(j) + count
+
+    @pl.loop(LAG, 2 * far + h + count)
     def _(t):
         jr = t - LAG * z
         jl = t - (far - LAG * z)
@@ -365,6 +368,15 @@
         gather_step(gr, high(gr), right, left, inner_end, first)
         use_step(gl, low(gl), inner_first)
         use_step(gr, high(gr), inner_end)
+        late_use = t - far - h - count
+
+        @pl.when(valid(late_use, first, h))
+        def _():
+            use(block(late_use))
+
+        @pl.when(valid(late_use, end, h))
+        def _():
+            use(block(late_use) + h)
 
     bits = [(u // (1 << i)) % 2 for i in range(levels)]
     partners = [u + (1 << i) * (1 - 2 * bits[i]) for i in range(levels)]
@@ -490,16 +502,16 @@
     for d in range(1, nu):
         cc_copy(d).wait_send()
 
-    @pl.loop(0, 2 * h)
+    @pl.loop(0, count)
     def _(c):
         @pl.when(z > 0)
         def _():
             a_copy(c, left).wait_send()
-            ag_copy(c + 2 * h, left).wait_send()
+            ag_copy(c + count, left).wait_send()
 
         @pl.when(z < ni - 1)
         def _():
-            a_copy(c + 2 * h, right).wait_send()
+            a_copy(c + count, right).wait_send()
             ag_copy(c, right).wait_send()
 
     @pl.loop(0, h)
@@ -527,7 +539,7 @@
         new_users, new_items = pl.pallas_call(
             functools.partial(kernel, nu, ni),
             out_shape=(
-                pltpu.VMEM((2 * ub, BLK // 2, k), f32),
+                pltpu.VMEM((PIECES * ub, BLK // PIECES, k), f32),
                 pltpu.VMEM((items, k), f32),
             ),
             in_specs=[hbm] * 5,
@@ -535,7 +547,7 @@
             scratch_shapes=[
                 pltpu.VMEM((ub, BLK, items), bf16),
                 pltpu.SMEM((ub, ib), jnp.int32),
-                pltpu.VMEM((2 * ub, BLK // 2, k), f32),
+                pltpu.VMEM((PIECES * ub, BLK // PIECES, k), f32),
                 pltpu.VMEM((items, k), f32),
                 pltpu.SMEM((2,), f32),
                 pltpu.VMEM((items, 2 * k), bf16),
@@ -544,10 +556,11 @@
                 pltpu.VMEM((-(-ub // 16) * 8, items), f32),
                 pltpu.VMEM((ub, k // 2 + 8, k), f32),
                 pltpu.VMEM((ub, k // 2 + 8, k), f32),
-                pltpu.VMEM((2 * ub, BLK // 2, k), f32),
-                pltpu.VMEM((2 * ub, BLK // 2, k), f32),
+                pltpu.VMEM((PIECES * ub, BLK // PIECES, k), f32),
+                pltpu.VMEM((PIECES * ub, BLK // PIECES, k), f32),
                 pltpu.VMEM((ub, 3 * k, k), bf16),
                 pltpu.VMEM((ub, 8, k), f32),
+                pltpu.VMEM((PIECES * ub, BLK // PIECES, k), f32),
                 pltpu.VMEM((2 * k, users), bf16),
                 pltpu.VMEM((ib, k, k), f32),
                 pltpu.VMEM((items, k), f32),
@@ -559,10 +572,10 @@
                 dma((ub,)),
                 dma((ub,)),
                 dma((ub,)),
-                dma((2 * ub,)),
-                dma((2 * ub,)),
-                dma((2 * ub,)),
-                dma((2 * ub,)),
+                dma((PIECES * ub,)),
+                dma((PIECES * ub,)),
+                dma((PIECES * ub,)),
+                dma((PIECES * ub,)),
                 dma((nu - 1,)),
                 dma((nu - 1,)),
                 dma((nu - 1,)),
@@ -576,7 +589,7 @@
             cost_estimate=pl.CostEstimate(
                 flops=8 * users * items * k, bytes_accessed=2 * users * items, transcendentals=0
             ),
-        )(ratings, presence, user_factors.reshape(2 * ub, BLK // 2, k), item_factors, step_sizes)
+        )(ratings, presence, user_factors.reshape(PIECES * ub, BLK // PIECES, k), item_factors, step_sizes)
         return new_users.reshape(users, k), new_items
 
     return jax.shard_map(

time: 52.3 us -> 52.2 us (level)
  no operation moved by 1% of the time
where the time goes in v6:
time: 52.2 us; the launch traced here: 52.1 us
  Pallas kernels  49.8 us (95%)
  local copies, waits for them, and re-layouts  1.63 us (3%)
  between operations  0.64 us (1%)
    pallas_call x1, Pallas kernels, body(): pl.pallas_call(functools.partial(kernel, nu, ni), out_shape=(pltpu.VMEM((...  49.8 us
    unnamed x2, local copies, waits for them, and re-layouts  1.63 us

profile of v6, /device:TPU:0, one launch (start us, length us, event | category | flops | bytes accessed | tf_op | source)
XLA Modules:
  0.0 52.1 jit_solution(14996621179417579011)
XLA Ops:
  0.6 49.8 %shard_map.68 = (f32[12,64,128]{2,1,0:T(8,128)S(1)}, f32[1536,128]{1,0:T(8,128)S(1)}) custom-call(bf16[768,1536]{1,0:T(8,128)(2,1)} %r_hbm.1, s32[6,12]{1,0:T(8,128)} %p_hbm.1, f32[12,64,128]{2,1,0:T(8,128)} %bitcast.3, f32[1536,128]{1,0:T(8,128)} %q_hbm.1, f32[2]{0:T(128)} %step_hbm.1), custom_call_target="tpu_custom_call" | custom-call | flops 1207959552 | bytes 2359296 | tf_op jit(solution)/shard_map/pallas_call | solution.py:539
  50.5 0.7 %copy.9 = f32[768,128]{1,0:T(8,128)} copy(f32[768,128]{1,0:T(8,128)S(1)} %bitcast.2) | data formatting | bytes 786432
  51.2 0.9 %copy.10 = f32[1536,128]{1,0:T(8,128)} copy(f32[1536,128]{1,0:T(8,128)S(1)} %get-tuple-element.7) | data formatting | bytes 1572864

commit v7 on v6

--- a/solution.py
+++ b/solution.py
@@ -298,34 +298,41 @@
     def valid(j, away, count):
         return jnp.logical_and(away, jnp.logical_and(j >= 0, j < count))
 
-    def g_step(j, b, frm, to, away, last):
-        @pl.when(valid(j, away, h))
-        def _():
-            g_copy(b, frm).wait_recv()
-            gpart[b] = gpart[b] + g_in[b]
-
-            @pl.when(jnp.logical_not(last))
+    def g_step(b, frm, to, last):
+        g_copy(b, frm).wait_recv()
+        gpart[b] = gpart[b] + g_in[b]
+
+        @pl.when(jnp.logical_not(last))
+        def _():
+            g_copy(b, to).start()
+
+        @pl.when(last)
+        def _():
+            prepare(b)
+
+    def a_step(c, frm, to, last):
+        a_copy(c, frm).wait_recv()
+        apart[c] = apart[c] + a_in[c]
+
+        @pl.when(jnp.logical_not(last))
+        def _():
+            a_copy(c, to).start()
+
+        @pl.when(last)
+        def _():
+            finish(c)
+            ag_copy(c, frm).start()
+
+    def reduce_step(j, base, frm, to, away, last):
+        @pl.when(valid(j, away, h + count))
+        def _():
+            @pl.when(j < h)
             def _():
-                g_copy(b, to).start()
-
-            @pl.when(last)
+                g_step(jnp.clip(j, 0, h - 1) + base * h, frm, to, last)
+
+            @pl.when(j >= h)
             def _():
-                prepare(b)
-
-    def a_step(j, c, frm, to, away, last):
-        @pl.when(valid(j, away, count))
-        def _():
-            a_copy(c, frm).wait_recv()
-            apart[c] = apart[c] + a_in[c]
-
-            @pl.when(jnp.logical_not(last))
-            def _():
-                a_copy(c, to).start()
-
-            @pl.when(last)
-            def _():
-                finish(c)
-                ag_copy(c, frm).start()
+                a_step(low(j - h) + base * count, frm, to, last)
 
     def gather_step(j, c, frm, to, away, last):
         @pl.when(valid(j, away, count))
@@ -345,38 +352,40 @@
     first, end = z == 0, z == ni - 1
     inner_first, inner_end = z > 0, z < ni - 1
 
-    def block(j):
-        return jnp.clip(j, 0, h - 1)
-
     def low(j):
         return jnp.clip(j, 0, count - 1)
 
     def high(j):
         return low(j) + count
 
-    @pl.loop(LAG, 2 * far + h + count)
+    @pl.loop(LAG, far + h + count)
     def _(t):
-        jr = t - LAG * z
-        jl = t - (far - LAG * z)
-        gl = t - far - h - LAG * z
-        gr = t - far - h - (far - LAG * z)
-        g_step(jr, block(jr) + h, left, right, inner_first, end)
-        g_step(jl, block(jl), right, left, inner_end, first)
-        a_step(jr - h, high(jr - h), left, right, inner_first, end)
-        a_step(jl - h, low(jl - h), right, left, inner_end, first)
+        reduce_step(t - LAG * z, 1, left, right, inner_first, end)
+        reduce_step(t - (far - LAG * z), 0, right, left, inner_end, first)
+
+    @pl.when(jnp.logical_or(first, end))
+    def _():
+        @pl.loop(0, h)
+        def _(n):
+            use(n + jnp.minimum(z, 1) * h)
+
+    for d in range(1, nu):
+        cc_copy(d).wait_recv()
+    counts = cc_out[...]
+    for d in range(1, nu):
+        counts = counts + cc_in[d - 1]
+    scaling = step_ref[1] / (BLK * (1.0 + counts))
+    for i in range(ib):
+        scale[i * BLK : (i + 1) * BLK, :] = jnp.broadcast_to(scaling[i : i + 1], (BLK, k))
+
+    @pl.loop(LAG, far + count)
+    def _(t):
+        gl = t - LAG * z
+        gr = t - (far - LAG * z)
         gather_step(gl, low(gl), left, right, inner_first, end)
         gather_step(gr, high(gr), right, left, inner_end, first)
         use_step(gl, low(gl), inner_first)
         use_step(gr, high(gr), inner_end)
-        late_use = t - far - h - count
-
-        @pl.when(valid(late_use, first, h))
-        def _():
-            use(block(late_use))
-
-        @pl.when(valid(late_use, end, h))
-        def _():
-            use(block(late_use) + h)
 
     bits = [(u // (1 << i)) % 2 for i in range(levels)]
     partners = [u + (1 << i) * (1 - 2 * bits[i]) for i in range(levels)]
@@ -464,15 +473,6 @@
     for f in (1, 0):
         second = 1 - mine[1] if f else mine[1]
         product(mine[0] * 2 * quarter + second * quarter, quarter)
-
-    for d in range(1, nu):
-        cc_copy(d).wait_recv()
-    counts = cc_out[...]
-    for d in range(1, nu):
-        counts = counts + cc_in[d - 1]
-    scaling = step_ref[1] / (BLK * (1.0 + counts))
-    for i in range(ib):
-        scale[i * BLK : (i + 1) * BLK, :] = jnp.broadcast_to(scaling[i : i + 1], (BLK, k))
 
     for level in range(levels):
         for tail in reversed(tails(level)):

time: 52.2 us -> 52.1 us (level)
  no operation moved by 1% of the time
where the time goes in v7:
time: 52.1 us; the launch traced here: 51.9 us
  Pallas kernels  49.7 us (95%)
  local copies, waits for them, and re-layouts  1.63 us (3%)
  between operations  0.64 us (1%)
    pallas_call x1, Pallas kernels, body(): pl.pallas_call(functools.partial(kernel, nu, ni), out_shape=(pltpu.VMEM((...  49.7 us
    unnamed x2, local copies, waits for them, and re-layouts  1.63 us

profile of v7, /device:TPU:0, one launch (start us, length us, event | category | flops | bytes accessed | tf_op | source)
XLA Modules:
  0.0 51.9 jit_solution(16960997575002664633)
XLA Ops:
  0.6 49.7 %shard_map.68 = (f32[12,64,128]{2,1,0:T(8,128)S(1)}, f32[1536,128]{1,0:T(8,128)S(1)}) custom-call(bf16[768,1536]{1,0:T(8,128)(2,1)} %r_hbm.1, s32[6,12]{1,0:T(8,128)} %p_hbm.1, f32[12,64,128]{2,1,0:T(8,128)} %bitcast.3, f32[1536,128]{1,0:T(8,128)} %q_hbm.1, f32[2]{0:T(128)} %step_hbm.1), custom_call_target="tpu_custom_call" | custom-call | flops 1207959552 | bytes 2359296 | tf_op jit(solution)/shard_map/pallas_call | solution.py:539
  50.3 0.7 %copy.9 = f32[768,128]{1,0:T(8,128)} copy(f32[768,128]{1,0:T(8,128)S(1)} %bitcast.2) | data formatting | bytes 786432
  51.1 0.9 %copy.10 = f32[1536,128]{1,0:T(8,128)} copy(f32[1536,128]{1,0:T(8,128)S(1)} %get-tuple-element.7) | data formatting | bytes 1572864

commit v8 on v7

--- a/solution.py
+++ b/solution.py
@@ -220,8 +220,7 @@
 
     pl.semaphore_wait(barrier, nu - 1 + jnp.minimum(z, 1) + jnp.minimum(ni - 1 - z, 1))
 
-    @pl.loop(0, 2)
-    def _(m):
+    def work_out(m):
         base = lax.rem(m + 1 - late, 2) * h
         for n in range(h):
             b = base + n
@@ -269,6 +268,8 @@
             for n in range(count):
                 a_copy(PIECES * base + n, right).start()
 
+    work_out(0)
+
     for d in range(1, nu):
         cc_copy(d).start()
 
@@ -358,10 +359,19 @@
     def high(j):
         return low(j) + count
 
+    turn = LAG * (ni // 2 - 1) + min(h, LAG) - 1
+    if turn < LAG:
+        work_out(1)
+
     @pl.loop(LAG, far + h + count)
     def _(t):
         reduce_step(t - LAG * z, 1, left, right, inner_first, end)
         reduce_step(t - (far - LAG * z), 0, right, left, inner_end, first)
+        if turn >= LAG:
+
+            @pl.when(t == turn)
+            def _():
+                work_out(1)
 
     @pl.when(jnp.logical_or(first, end))
     def _():
@@ -470,12 +480,11 @@
         for tail in reversed(tails(0)):
             if tail[0] == f:
                 half_copy(0, tail).start()
-    for f in (1, 0):
-        second = 1 - mine[1] if f else mine[1]
-        product(mine[0] * 2 * quarter + second * quarter, quarter)
-
     for level in range(levels):
         for tail in reversed(tails(level)):
+            if level == 0 and all(tail[1:]):
+                second = 1 - mine[1] if tail[0] else mine[1]
+                product(mine[0] * 2 * quarter + second * quarter, quarter)
             half_copy(level, tail).wait_recv()
             rows = held(level, tail)
             summed = acc[rows, :] + halves[place(level, tail)]

time: 52.1 us -> 51.8 us (level)
  no operation moved by 1% of the time
where the time goes in v8:
time: 51.8 us; the launch traced here: 51.6 us
  Pallas kernels  49.4 us (95%)
  local copies, waits for them, and re-layouts  1.63 us (3%)
  between operations  0.64 us (1%)
    pallas_call x1, Pallas kernels, body(): pl.pallas_call(functools.partial(kernel, nu, ni), out_shape=(pltpu.VMEM((...  49.4 us
    unnamed x2, local copies, waits for them, and re-layouts  1.63 us

profile of v8, /device:TPU:0, one launch (start us, length us, event | category | flops | bytes accessed | tf_op | source)
XLA Modules:
  0.0 51.6 jit_solution(14257337085229497492)
XLA Ops:
  0.6 49.4 %shard_map.68 = (f32[12,64,128]{2,1,0:T(8,128)S(1)}, f32[1536,128]{1,0:T(8,128)S(1)}) custom-call(bf16[768,1536]{1,0:T(8,128)(2,1)} %r_hbm.1, s32[6,12]{1,0:T(8,128)} %p_hbm.1, f32[12,64,128]{2,1,0:T(8,128)} %bitcast.3, f32[1536,128]{1,0:T(8,128)} %q_hbm.1, f32[2]{0:T(128)} %step_hbm.1), custom_call_target="tpu_custom_call" | custom-call | flops 1207959552 | bytes 2359296 | tf_op jit(solution)/shard_map/pallas_call | solution.py:548
  50.0 0.7 %copy.9 = f32[768,128]{1,0:T(8,128)} copy(f32[768,128]{1,0:T(8,128)S(1)} %bitcast.2) | data formatting | bytes 786432
  50.7 0.9 %copy.10 = f32[1536,128]{1,0:T(8,128)} copy(f32[1536,128]{1,0:T(8,128)S(1)} %get-tuple-element.7) | data formatting | bytes 1572864

commit v9 on v8

--- a/solution.py
+++ b/solution.py
@@ -10,7 +10,7 @@
 
 BLK = 128
 PIECES = 2
-LAG = 3
+LAG = 5
 f32 = jnp.float32
 bf16 = jnp.bfloat16
 MESH = pl.DeviceIdType.MESH

time: 51.8 us -> 50.8 us (0.981)
  Pallas kernels: 49.4 us -> 48.4 us
    pallas_call x1, Pallas kernels: 49.4 us -> 48.4 us  [body(): pl.pallas_call(functools.partial(kernel, nu, ni), out_shape=(pltpu.VMEM((...]
where the time goes in v9:
time: 50.8 us; the launch traced here: 50.6 us
  Pallas kernels  48.4 us (95%)
  local copies, waits for them, and re-layouts  1.63 us (3%)
  between operations  0.64 us (1%)
    pallas_call x1, Pallas kernels, body(): pl.pallas_call(functools.partial(kernel, nu, ni), out_shape=(pltpu.VMEM((...  48.4 us
    unnamed x2, local copies, waits for them, and re-layouts  1.63 us

profile of v9, /device:TPU:0, one launch (start us, length us, event | category | flops | bytes accessed | tf_op | source)
XLA Modules:
  0.0 50.6 jit_solution(2888494812141950838)
XLA Ops:
  0.6 48.4 %shard_map.68 = (f32[12,64,128]{2,1,0:T(8,128)S(1)}, f32[1536,128]{1,0:T(8,128)S(1)}) custom-call(bf16[768,1536]{1,0:T(8,128)(2,1)} %r_hbm.1, s32[6,12]{1,0:T(8,128)} %p_hbm.1, f32[12,64,128]{2,1,0:T(8,128)} %bitcast.3, f32[1536,128]{1,0:T(8,128)} %q_hbm.1, f32[2]{0:T(128)} %step_hbm.1), custom_call_target="tpu_custom_call" | custom-call | flops 1207959552 | bytes 2359296 | tf_op jit(solution)/shard_map/pallas_call | solution.py:548
  49.0 0.7 %copy.9 = f32[768,128]{1,0:T(8,128)} copy(f32[768,128]{1,0:T(8,128)S(1)} %bitcast.2) | data formatting | bytes 786432
  49.8 0.9 %copy.10 = f32[1536,128]{1,0:T(8,128)} copy(f32[1536,128]{1,0:T(8,128)S(1)} %get-tuple-element.7) | data formatting | bytes 1572864

commit v10 on v9

--- a/solution.py
+++ b/solution.py
@@ -10,7 +10,7 @@
 
 BLK = 128
 PIECES = 2
-LAG = 5
+LAG = 7
 f32 = jnp.float32
 bf16 = jnp.bfloat16
 MESH = pl.DeviceIdType.MESH

time: 50.8 us -> 51.4 us (1.012)
  Pallas kernels: 48.4 us -> 49 us
    pallas_call x1, Pallas kernels: 48.4 us -> 49 us  [body(): pl.pallas_call(functools.partial(kernel, nu, ni), out_shape=(pltpu.VMEM((...]
where the time goes in v10:
time: 51.4 us; the launch traced here: 51.2 us
  Pallas kernels  49 us (95%)
  local copies, waits for them, and re-layouts  1.63 us (3%)
  between operations  0.64 us (1%)
    pallas_call x1, Pallas kernels, body(): pl.pallas_call(functools.partial(kernel, nu, ni), out_shape=(pltpu.VMEM((...  49 us
    unnamed x2, local copies, waits for them, and re-layouts  1.63 us

profile of v10, /device:TPU:0, one launch (start us, length us, event | category | flops | bytes accessed | tf_op | source)
XLA Modules:
  0.0 51.2 jit_solution(14958649443531776966)
XLA Ops:
  0.6 49.0 %shard_map.68 = (f32[12,64,128]{2,1,0:T(8,128)S(1)}, f32[1536,128]{1,0:T(8,128)S(1)}) custom-call(bf16[768,1536]{1,0:T(8,128)(2,1)} %r_hbm.1, s32[6,12]{1,0:T(8,128)} %p_hbm.1, f32[12,64,128]{2,1,0:T(8,128)} %bitcast.3, f32[1536,128]{1,0:T(8,128)} %q_hbm.1, f32[2]{0:T(128)} %step_hbm.1), custom_call_target="tpu_custom_call" | custom-call | flops 1207959552 | bytes 2359296 | tf_op jit(solution)/shard_map/pallas_call | solution.py:548
  49.6 0.7 %copy.9 = f32[768,128]{1,0:T(8,128)} copy(f32[768,128]{1,0:T(8,128)S(1)} %bitcast.2) | data formatting | bytes 786432
  50.4 0.9 %copy.10 = f32[1536,128]{1,0:T(8,128)} copy(f32[1536,128]{1,0:T(8,128)S(1)} %get-tuple-element.7) | data formatting | bytes 1572864
